TPU v7x, 32 devices: a whole 2x2x4 slice. The times are simulated.
32 devices in a mesh: req: 2 (over y), ctx: 4 (over x, core), tp: 4 (over z).
Axes of the slice: x: 2, y: 2, z: 4, core: 2. Of those that a mesh axis runs over, the one named last changes fastest.
Arguments:
- hidden_in: bfloat16 [4096, 6144], P(('req', 'ctx', 'tp')), parts along dimension 0, may hold values from -5 to 5
- queries: bfloat16 [4096, 4096], P(('req', 'ctx', 'tp')), parts along dimension 0, may hold values from -40 to 40
- keys: bfloat16 [4096, 1024], P(('req', 'ctx', 'tp')), parts along dimension 0, may hold values from -8 to 8
- values: bfloat16 [4096, 1024], P(('req', 'ctx', 'tp')), parts along dimension 0, may hold values from -6 to 6
- block_order: int32 [8], P('req'), parts along dimension 0, may hold values from 0 to 3, each once
- routes: int32 [4096, 2], P(('req', 'ctx')), parts along dimension 0, may hold values from 0 to 7, as said below
- out_weight: bfloat16 [4096, 6144], P('tp'), may hold values from -0.09375 to 0.09375
- norm_gain: float32 [6144], replicated, may hold values from 0.1 to 1.9
- router_weight: bfloat16 [6144, 8], replicated, may hold values from -0.078125 to 0.078125
- gate_weight: bfloat16 [6144, 8192], P(None, 'tp'), may hold values from -0.078125 to 0.078125
- up_weight: bfloat16 [6144, 8192], P(None, 'tp'), may hold values from -0.078125 to 0.078125
- down_weight: bfloat16 [8192, 6144], P('tp'), may hold values from -0.0625 to 0.0625
Outputs:
- attended: bfloat16 [4096, 6144], P(('req', 'ctx', 'tp')), parts along dimension 0
- expert_out: bfloat16 [4096, 6144], P(('req', 'ctx', 'tp')), parts along dimension 0
There are 2 independent parts, one for each index of `req`. A program takes and returns all parts, laid end to end along the dimension named above; an argument that names none is the same for every part. Nothing has to cross between parts.
Inputs may be any that keep to these rules, and one draw needn't show every extreme that they name: `routes`: each row names two different experts. In each block of 512 rows at most 192 rows name expert 0, and exactly 192 in at least one block.
All inputs are finite; a program needn't handle non-finite values.
Results may differ from a plain program's by a relative error of at most 0.023.
Values may be sent and summed in bfloat16 or wider, within the bound.
No kernel may reach another device: no remote copies, remote signals or barrier semaphores. Data moves between devices by JAX's collectives and lax.ppermute only.
A program may use at most 256 MiB of HBM per device.

v0:
```python
import functools
import math

import jax
import jax.numpy as jnp
from jax import lax
from jax.experimental import pallas as pl
from jax.experimental.pallas import tpu as pltpu
from jax.sharding import PartitionSpec as P

HEADS = 32
KV_HEADS = 8
HD = 128
FACTOR = math.log2(math.e) / math.sqrt(HD)
LINE = 4
SUM_ROWS = 16
TILE = 256


def attention_kernel(slots, held, pairs, sharing, block_rows, *refs):
    (order, mine), refs = refs[:2], refs[2:]
    query_refs, refs = refs[:slots], refs[slots:]
    place_ref, key_place_ref, refs = refs[0], refs[1], refs[2:]
    pair_refs, refs = refs[: len(held)], refs[len(held) :]
    out_ref, query_ref, value_ref, top_ref, total_ref = refs
    half = out_ref.shape[1]
    me = mine[0]
    my_block = order[me]
    blocks = [(ref, index, offset) for ref, group in zip(pair_refs, held) for index, offset in enumerate(group)]

    @pl.when(pl.program_id(0) == 0)
    def _():
        value_ref[:, :, HD:, :] = jnp.ones((len(blocks), pairs, SUM_ROWS, block_rows), jnp.bfloat16)

    for at, (ref, index, offset) in enumerate(blocks):

        @pl.when((pl.program_id(0) == 0) & (order[me ^ offset] <= my_block))
        def _():
            for p in range(pairs):
                columns = slice((pairs + p) * HD, (pairs + p + 1) * HD)
                value_ref[at, p, :HD, :] = ref[index * block_rows : (index + 1) * block_rows, columns].T

    for at in range(slots):

        @pl.when(pl.program_id(0) == at)
        def _():
            for p in range(pairs):
                for g in range(sharing):
                    column = (p * sharing + g) * HD
                    query_ref[p, g * half : (g + 1) * half, :] = query_refs[at][:, column : column + HD]

    def scores_of(p, at):
        ref, index, _ = blocks[at]
        key = ref[index * block_rows : (index + 1) * block_rows, p * HD : (p + 1) * HD]
        return lax.dot_general(
            key, query_ref[p], (((1,), (1,)), ((), ())), preferred_element_type=jnp.float32
        )

    def mixed_of(p, at, weights):
        return jnp.dot(value_ref[at, p], weights, preferred_element_type=jnp.float32)

    place = jnp.concatenate([place_ref[0]] * sharing, axis=1)
    visible = key_place_ref[...] <= place
    for p in range(pairs):
        scores = jnp.where(visible, scores_of(p, 0), -1e30)
        top = jnp.max(scores, axis=0, keepdims=True)
        weights = jnp.exp2((scores - top) * FACTOR).astype(jnp.bfloat16)
        top_ref[p, 0:1, :] = top
        total_ref[p] = mixed_of(p, 0, weights)

    for at in range(1, len(blocks)):

        @pl.when(order[me ^ blocks[at][2]] < my_block)
        def _():
            for p in range(pairs):
                top = top_ref[p, 0:1, :]
                scores = scores_of(p, at)
                raised = jnp.maximum(top, jnp.max(scores, axis=0, keepdims=True))
                weights = jnp.exp2((scores - raised) * FACTOR).astype(jnp.bfloat16)
                top_ref[p, 0:1, :] = raised
                total_ref[p] = total_ref[p] * jnp.exp2((top - raised) * FACTOR) + mixed_of(p, at, weights)

    for p in range(pairs):
        mixed = (total_ref[p, :HD, :] / total_ref[p, HD : HD + 1, :]).T.astype(jnp.bfloat16)
        for g in range(sharing):
            column = (p * sharing + g) * HD
            out_ref[0, :, column : column + HD] = mixed[g * half : (g + 1) * half]


def attend(order, mine, queries, places, key_places, pair_list, held, pairs, sharing, block_rows):
    slots = len(queries)
    half, width = queries[0].shape
    tall = sharing * half
    blocks = sum(len(group) for group in held)
    count = blocks * block_rows
    kernel = functools.partial(attention_kernel, slots, held, pairs, sharing, block_rows)
    whole = [pl.BlockSpec(pair.shape, lambda s, *_: (0, 0)) for pair in pair_list]
    return pl.pallas_call(
        kernel,
        grid_spec=pltpu.PrefetchScalarGridSpec(
            num_scalar_prefetch=2,
            grid=(slots,),
            in_specs=[pl.BlockSpec((half, width), lambda s, *_: (0, 0))] * slots
            + [
                pl.BlockSpec((1, 1, half), lambda s, *_: (s, 0, 0)),
                pl.BlockSpec((block_rows, 1), lambda s, *_: (0, 0)),
            ]
            + whole,
            out_specs=pl.BlockSpec((1, half, width), lambda s, *_: (s, 0, 0)),
            scratch_shapes=[
                pltpu.VMEM((pairs, tall, HD), jnp.bfloat16),
                pltpu.VMEM((blocks, pairs, HD + SUM_ROWS, block_rows), jnp.bfloat16),
                pltpu.VMEM((pairs, 8, tall), jnp.float32),
                pltpu.VMEM((pairs, HD + SUM_ROWS, tall), jnp.float32),
            ],
        ),
        out_shape=jax.ShapeDtypeStruct((slots, half, width), jnp.bfloat16),
        compiler_params=pltpu.CompilerParams(vmem_limit_bytes=24 * 1024 * 1024),
        cost_estimate=pl.CostEstimate(
            flops=4 * slots * half * width * count,
            bytes_accessed=2 * (2 * slots * half * width + count * 2 * pairs * HD),
            transcendentals=slots * half * width // HD * count,
        ),
    )(order, mine, *queries, places, key_places, *pair_list)


def hidden_kernel(plan, started, last, streams, *refs):
    mine, refs = refs[0], refs[1:]
    sources, refs = refs[:plan], refs[plan:]
    gate_weights, up_weights, refs = refs[:streams], refs[streams : 2 * streams], refs[2 * streams :]
    if started:
        gate_before, up_before, refs = refs[0], refs[1], refs[2:]
    if last:
        out, chosen, gate, upward = refs
    else:
        gate, upward, chosen = refs
    step = pl.program_id(0)
    steps = pl.num_programs(0)
    tile = gate_weights[0].shape[0]

    @pl.when(step == 0)
    def _():
        if plan == 1:
            chosen[...] = sources[0][...]
        else:
            shards = (plan + 1) // 2
            rows = sources[0].shape[0]
            chosen[:rows] = sources[0][...]
            for s in range(1, shards):
                right, left = sources[s], sources[plan - s]

                @pl.when(mine[0] >= s)
                def _():
                    chosen[s * rows : (s + 1) * rows] = right[...]

                @pl.when(mine[0] < s)
                def _():
                    chosen[s * rows : (s + 1) * rows] = left[...]

    parts = []
    for weights in (gate_weights, up_weights):
        total = None
        for j, weight in enumerate(weights):
            columns = pl.ds(pl.multiple_of((j * steps + step) * tile, tile), tile)
            term = jnp.dot(chosen[:, columns], weight[...], preferred_element_type=jnp.float32)
            total = term if total is None else total + term
        parts.append(total)

    @pl.when(step == 0)
    def _():
        gate[...] = parts[0] + gate_before[...] if started else parts[0]
        upward[...] = parts[1] + up_before[...] if started else parts[1]

    @pl.when(step > 0)
    def _():
        gate[...] += parts[0]
        upward[...] += parts[1]

    if last:

        @pl.when(step == steps - 1)
        def _():
            value = gate[...]
            out[...] = (value / (1.0 + jnp.exp(-value)) * upward[...]).astype(jnp.bfloat16)


def hidden_units(mine, sources, gate_weight, up_weight, cut, before, last):
    shards = (len(sources) + 1) // 2
    rows = sources[0].shape[0] * shards
    depth = sources[0].shape[1]
    width = gate_weight.shape[1]
    tile, streams = TILE, 2
    steps = depth // (tile * streams)
    weights = [
        pl.BlockSpec((tile, width), functools.partial(lambda j, k, *_: ((cut * streams + j) * steps + k, 0), j))
        for j in range(streams)
    ]
    out = pl.BlockSpec((rows, width), lambda k, *_: (0, 0))
    kinds = [jnp.bfloat16] if last else [jnp.float32] * 2
    scratch = [pltpu.VMEM((rows, depth), jnp.bfloat16)]
    if last:
        scratch += [pltpu.VMEM((rows, width), jnp.float32)] * 2
    return pl.pallas_call(
        functools.partial(hidden_kernel, len(sources), len(before) > 0, last, streams),
        grid_spec=pltpu.PrefetchScalarGridSpec(
            num_scalar_prefetch=1,
            grid=(steps,),
            in_specs=[pl.BlockSpec(source.shape, lambda k, *_: (0, 0)) for source in sources]
            + weights
            + weights
            + [out] * len(before),
            out_specs=[out] * len(kinds),
            scratch_shapes=scratch,
        ),
        out_shape=[jax.ShapeDtypeStruct((rows, width), kind) for kind in kinds],
        compiler_params=pltpu.CompilerParams(vmem_limit_bytes=40 * 1024 * 1024),
        cost_estimate=pl.CostEstimate(
            flops=4 * rows * depth * width, bytes_accessed=4 * depth * width, transcendentals=rows * width
        ),
    )(mine, *sources, *[gate_weight] * streams, *[up_weight] * streams, *before)


def product_kernel(streams, left_ref, *refs):
    weights, (out_ref, total) = refs[:streams], refs[streams:]
    step = pl.program_id(0)
    steps = pl.num_programs(0)
    tile = weights[0].shape[0]
    value = None
    for j, weight in enumerate(weights):
        columns = pl.ds(pl.multiple_of((j * steps + step) * tile, tile), tile)
        term = jnp.dot(left_ref[:, columns], weight[...], preferred_element_type=jnp.float32)
        value = term if value is None else value + term

    @pl.when(step == 0)
    def _():
        total[...] = value

    @pl.when(step > 0)
    def _():
        total[...] += value

    @pl.when(step == steps - 1)
    def _():
        out_ref[...] = total[...].astype(jnp.bfloat16)


def product(left, weight, cut, pieces):
    rows, depth = left.shape
    width = weight.shape[1] // pieces
    tile = min(TILE, depth)
    streams = 2 if depth % (2 * tile) == 0 else 1
    steps = depth // (tile * streams)
    return pl.pallas_call(
        functools.partial(product_kernel, streams),
        grid=(steps,),
        in_specs=[pl.BlockSpec((rows, depth), lambda k: (0, 0))]
        + [
            pl.BlockSpec((tile, width), functools.partial(lambda j, k: (j * steps + k, cut), j))
            for j in range(streams)
        ],
        out_specs=pl.BlockSpec((rows, width), lambda k: (0, 0)),
        out_shape=jax.ShapeDtypeStruct((rows, width), jnp.bfloat16),
        scratch_shapes=[pltpu.VMEM((rows, width), jnp.float32)],
        compiler_params=pltpu.CompilerParams(vmem_limit_bytes=40 * 1024 * 1024),
        cost_estimate=pl.CostEstimate(
            flops=2 * rows * depth * width, bytes_accessed=2 * depth * width, transcendentals=0
        ),
    )(left, *[weight] * streams)


def pack_pairs_kernel(shards, mine, keys_ref, values_ref, *outs):
    width = keys_ref.shape[1] // shards
    for s in range(shards):
        columns = pl.ds(pl.multiple_of(lax.rem(mine[0] + s, shards) * width, width), width)
        outs[s][:, :width] = keys_ref[:, columns]
        outs[s][:, width:] = values_ref[:, columns]


def pack_pairs(mine, keys, values, shards):
    rows, width = keys.shape
    spec = pl.BlockSpec((rows, width), lambda k, *_: (0, 0))
    out = (rows, 2 * width // shards)
    return pl.pallas_call(
        functools.partial(pack_pairs_kernel, shards),
        grid_spec=pltpu.PrefetchScalarGridSpec(
            num_scalar_prefetch=1,
            grid=(1,),
            in_specs=[spec, spec],
            out_specs=[pl.BlockSpec(out, lambda k, *_: (0, 0))] * shards,
        ),
        out_shape=[jax.ShapeDtypeStruct(out, keys.dtype)] * shards,
    )(mine, keys, values)


def pack_queries_kernel(shards, halves, mine, picked_ref, query_ref, *outs):
    rows = query_ref.shape[0]
    half = rows // halves
    width = query_ref.shape[1] // shards
    packed, (order_ref, places_ref, count_ref) = outs[: halves * shards], outs[halves * shards :]
    me = mine[0]
    across = lax.broadcasted_iota(jnp.int32, (rows, rows), 1)
    down = lax.broadcasted_iota(jnp.int32, (rows, rows), 0)
    up_to = jnp.where(down <= across, 1.0, 0.0).astype(jnp.bfloat16)
    picked = picked_ref[...]
    seen = jnp.dot(picked.astype(jnp.bfloat16), up_to, preferred_element_type=jnp.float32).astype(jnp.int32)
    count = seen[:, rows - 1 : rows]
    row_ids = lax.broadcasted_iota(jnp.int32, seen.shape, 1)
    slot = jnp.where(picked > 0, seen - 1, count + row_ids - seen)
    count_ref[...] = jnp.broadcast_to(jnp.max(count, axis=0, keepdims=True), count_ref.shape).astype(jnp.float32)
    ids = row_ids.astype(jnp.bfloat16)
    for s in range(shards):
        shard = lax.rem(me - s + shards, shards)
        mine_slot = slot[0:1]
        for other in range(1, shards):
            mine_slot = jnp.where(shard == other, slot[other : other + 1], mine_slot)
        at_slot = jnp.where(mine_slot == down, 1.0, 0.0).astype(jnp.bfloat16)
        rows_at = lax.dot_general(ids, at_slot, (((1,), (1,)), ((), ())), preferred_element_type=jnp.float32)
        places_ref[s] = rows_at[0:1].astype(jnp.int32) + shard * rows
        if s == 0:
            order_ref[...] = at_slot
    for s in range(shards):
        columns = pl.ds(pl.multiple_of(lax.rem(me + s, shards) * width, width), width)
        ordered = jnp.dot(order_ref[...], query_ref[:, columns], preferred_element_type=jnp.float32)
        ordered = ordered.astype(jnp.bfloat16)
        for h in range(halves):
            packed[h * shards + s][...] = ordered[h * half : (h + 1) * half]


def pack_queries(mine, picked, queries, shards, halves):
    rows, width = queries.shape
    packed = (rows // halves, width // shards)
    shapes = [jax.ShapeDtypeStruct(packed, jnp.bfloat16)] * (halves * shards) + [
        jax.ShapeDtypeStruct((rows, rows), jnp.bfloat16),
        jax.ShapeDtypeStruct((shards, 1, rows), jnp.int32),
        jax.ShapeDtypeStruct((8, 128), jnp.float32),
    ]

    def whole(shape):
        return pl.BlockSpec(shape, lambda k, *_: (0,) * len(shape))

    got = pl.pallas_call(
        functools.partial(pack_queries_kernel, shards, halves),
        grid_spec=pltpu.PrefetchScalarGridSpec(
            num_scalar_prefetch=1,
            grid=(1,),
            in_specs=[whole(picked.shape), whole(queries.shape)],
            out_specs=[whole(shape.shape) for shape in shapes],
        ),
        out_shape=shapes,
    )(mine, picked, queries)
    return [got[h * shards : (h + 1) * shards] for h in range(halves)], *got[halves * shards :]


def on_device(
    hidden_in,
    queries,
    keys,
    values,
    block_order,
    routes,
    out_weight,
    norm_gain,
    router_weight,
    gate_weight,
    up_weight,
    down_weight,
):
    shards = lax.axis_size("tp")
    blocks = lax.axis_size("ctx")
    me = lax.axis_index("tp")
    rows, model = hidden_in.shape
    block_rows = rows * shards
    per_device = HEADS // shards
    grouping = HEADS // KV_HEADS
    repeat_by = max(1, grouping // per_device)
    pairs = max(1, per_device // grouping)
    sharing = per_device // pairs
    half = rows // 2 if rows % 32 == 0 else rows
    halves = rows // half
    line = shards <= LINE
    pieces = 2 if line else 1
    cuts = [slice(c * (model // pieces), (c + 1) * (model // pieces)) for c in range(pieces)]
    shard_of = lax.rem(me - jnp.arange(shards, dtype=jnp.int32) + shards, shards)

    def shift(parts):
        moves = [[(i, (i + s) % shards) for i in range(shards)] for s in range(shards)]
        return [parts[0]] + [lax.ppermute(parts[s], "tp", moves[s]) for s in range(1, shards)]

    def exchange(source):
        got = lax.all_to_all(source, "tp", split_axis=1, concat_axis=0, tiled=True)
        got = got.reshape(shards, rows, source.shape[2])
        return [lax.dynamic_index_in_dim(got, shard_of[s], 0, keepdims=False) for s in range(shards)]

    def rights(count):
        return [(i, i + 1) for i in range(count)]

    def lefts(count):
        return [(i, i - 1) for i in range(shards - count, shards)]

    def reduce_line(terms):
        if not line:
            by_shard = jnp.take(jnp.stack(terms), shard_of, axis=0).reshape(-1, terms[0].shape[1])
            return lax.psum_scatter(by_shard, "tp", scatter_dimension=0, tiled=True).astype(jnp.float32), None
        right = left = mark = None
        for s in range(1, shards):
            to_right, to_left = terms[s], terms[shards - s]
            if right is not None:
                to_right = to_right + right
                to_left = to_left + left
            right = lax.ppermute(to_right, "tp", rights(s))
            left = lax.ppermute(to_left, "tp", lefts(s))
            right, left = lax.optimization_barrier((right, left))
            mark = right if mark is None else mark
        return terms[0].astype(jnp.float32) + right.astype(jnp.float32) + left.astype(jnp.float32), mark

    def gather_line(source, terms=None):
        if not line:
            got = lax.all_gather(source, "tp", axis=0)
            return [jnp.take(got, shard_of, axis=0).reshape(shards * half, -1)], None
        right = left = source
        from_left, from_right = [], []
        for s in range(1, shards):
            if s > 1 and terms is not None:
                right = jnp.where(me >= s - 1, right, right + terms[s - 1])
                left = jnp.where(me <= shards - s, left, left + terms[shards - s + 1])
            if s == 1 or terms is not None:
                to_right, to_left = rights(shards - 1), lefts(shards - 1)
            else:
                to_right = [(i, i + 1) for i in range(s - 1, shards - 1)]
                to_left = [(i, i - 1) for i in range(1, shards - s + 1)]
            right = lax.ppermute(right, "tp", to_right)
            left = lax.ppermute(left, "tp", to_left)
            right, left = lax.optimization_barrier((right, left))
            from_left.append(right)
            from_right.append(left)
        total = None
        if terms is not None:
            right = lax.ppermute(right + terms[shards - 1], "tp", rights(shards - 1))
            left = lax.ppermute(left + terms[1], "tp", lefts(shards - 1))
            total = terms[0].astype(jnp.float32) + right.astype(jnp.float32) + left.astype(jnp.float32)
        return [source] + from_left + from_right, total

    key_places = (shard_of[:, None] * rows + jnp.arange(rows, dtype=jnp.int32)[None, :]).reshape(block_rows, 1)
    picked = ((routes[:, 0] == 0) | (routes[:, 1] == 0)).reshape(shards, rows)
    if line:
        sent_pairs = pack_pairs(me[None], keys, values, shards)
        own_pairs = jnp.concatenate(shift(sent_pairs), axis=0)
        picked, _ = lax.optimization_barrier((picked.astype(jnp.int32), sent_pairs))
        packed, order, places, fullest = pack_queries(me[None], picked, queries, shards, halves)
        asked = [shift(packed[h]) for h in range(halves)]
    else:

        def spread(source):
            widened = jnp.repeat(source.reshape(rows, KV_HEADS, HD), repeat_by, axis=1)
            return widened.reshape(rows, shards, pairs * HD)

        own_pairs = exchange(jnp.concatenate([spread(keys), spread(values)], axis=2))
        own_pairs = jnp.concatenate(own_pairs, axis=0)
        row_ids = jnp.arange(rows, dtype=jnp.int32)
        seen = jnp.cumsum(picked.astype(jnp.int32), axis=1)
        slot = jnp.where(picked, seen - 1, seen[:, -1:] + row_ids[None, :] - seen)
        at_slot = slot[:, None, :] == row_ids[None, :, None]
        row_of_slot = jnp.sum(jnp.where(at_slot, row_ids[None, None, :], 0), axis=2)
        places = row_of_slot + jnp.arange(shards, dtype=jnp.int32)[:, None] * rows
        places = jnp.take(places, shard_of, axis=0)[:, None, :]
        order = lax.dynamic_index_in_dim(at_slot, me, 0, keepdims=False).astype(jnp.bfloat16)
        ordered = jnp.dot(order, queries, preferred_element_type=jnp.float32).astype(jnp.bfloat16)
        asked = [exchange(ordered.reshape(rows, shards, per_device * HD))]

    pair_list, held = [own_pairs], [[0]]
    offset = blocks // 2
    while offset >= 1:
        pair_list += [lax.ppermute(part, "ctx", [(i, i ^ offset) for i in range(blocks)]) for part in pair_list]
        held += [[other ^ offset for other in group] for group in held]
        offset //= 2

    def reorder(source):
        return jnp.dot(order, source, preferred_element_type=jnp.float32).astype(jnp.bfloat16)

    def restore(parts):
        whole = jnp.concatenate(parts, axis=0) if len(parts) > 1 else parts[0]
        return lax.dot_general(
            order, whole, (((0,), (0,)), ((), ())), preferred_element_type=jnp.float32
        ).astype(jnp.bfloat16)

    mine = lax.axis_index("ctx").astype(jnp.int32)[None]
    expert_ids = jnp.arange(router_weight.shape[1], dtype=jnp.int32)
    slots = [s for s in range(1, shards, 2)] + [s for s in range(2, shards, 2)] + [0]

    def project(which):
        heads = attend(
            block_order,
            mine,
            [asked[which][s] for s in slots],
            jnp.stack([places[s, :, which * half : (which + 1) * half] for s in slots]),
            key_places,
            pair_list,
            held,
            pairs,
            sharing,
            block_rows,
        ).reshape(shards * half, per_device * HD)
        terms = []
        for c in range(pieces):
            term = product(heads, out_weight, c, pieces)
            terms.append([term[slots.index(s) * half : (slots.index(s) + 1) * half] for s in range(shards)])
        return terms

    def finish(which, head_sums):
        base = hidden[which * half : (which + 1) * half].astype(jnp.float32)
        return jnp.concatenate(
            [(base[:, cut] + head_sum).astype(jnp.bfloat16) for cut, head_sum in zip(cuts, head_sums)], axis=1
        )

    def activate(attended, terms=None):
        widened = attended.astype(jnp.float32)
        normed = (
            widened * lax.rsqrt(jnp.mean(widened * widened, axis=1, keepdims=True) + 1e-05) * norm_gain
        ).astype(jnp.bfloat16)
        before = []
        sums = []
        for c, cut in enumerate(cuts):
            sources, total = gather_line(normed[:, cut], None if terms is None else terms[c])
            sums.append(total)
            before = hidden_units(me[None], sources, gate_weight, up_weight, c, before, c == pieces - 1)
        return normed, before[0], sums

    def share_of(which, normed):
        logits = jnp.dot(normed, router_weight, preferred_element_type=jnp.float32)
        named = my_routes[which * half : (which + 1) * half]
        first = jnp.sum(jnp.where(named[:, 0:1] == expert_ids[None, :], logits, 0.0), axis=1)
        second = jnp.sum(jnp.where(named[:, 1:2] == expert_ids[None, :], logits, 0.0), axis=1)
        share = jnp.where(named[:, 0] == 0, 1.0 / (1.0 + jnp.exp(second - first)), 0.0)
        return share + jnp.where(named[:, 1] == 0, 1.0 / (1.0 + jnp.exp(first - second)), 0.0)

    def deliver(acts, share):
        parts = []
        for c in range(pieces):
            term = product(acts, down_weight, c, pieces).reshape(shards, half, -1)
            total, _ = reduce_line([term[s] for s in range(shards)])
            parts.append((total * share[:, None]).astype(jnp.bfloat16))
        return jnp.concatenate(parts, axis=1)

    def late_expert(source):
        normed, acts, _ = activate(source)
        return deliver(acts, share_of(1, normed))

    reduced = [reduce_line(terms) for terms in project(0)]
    if line:
        asked[-1], hidden_in, order, fullest, _ = lax.optimization_barrier(
            (asked[-1], hidden_in, order, fullest, reduced[0][1])
        )
    hidden = reorder(hidden_in)
    my_routes = lax.dynamic_slice_in_dim(routes, me * rows, rows, 0).astype(jnp.bfloat16)
    my_routes = reorder(my_routes).astype(jnp.int32)
    totals = [total for total, _ in reduced]
    if halves == 1:
        first_half = finish(0, totals)
        normed, acts, _ = activate(first_half)
        return (restore([first_half]), restore([deliver(acts, share_of(0, normed))]))
    for axis in ("req", "ctx"):
        size = lax.axis_size(axis)
        step = 1
        while step < size:
            fullest = jnp.maximum(fullest, lax.ppermute(fullest, axis, [(i, i ^ step) for i in range(size)]))
            step *= 2
    terms = project(1)
    totals, terms, fullest = lax.optimization_barrier((totals, terms, fullest))
    first_half = finish(0, totals)
    normed, acts, sums = activate(first_half, terms)
    share = share_of(0, normed)
    second_half = finish(1, sums)
    acts, second_half = lax.optimization_barrier((acts, second_half))
    part = deliver(acts, share)
    part, late = lax.optimization_barrier((part, second_half))
    late = lax.cond(fullest[0, 0] > half, late_expert, jnp.zeros_like, late)
    return (restore([first_half, second_half]), restore([part, late]))


def solution(mesh):
    return jax.shard_map(
        on_device,
        mesh=mesh,
        in_specs=(
            P(("req", "ctx", "tp"), None),
            P(("req", "ctx", "tp"), None),
            P(("req", "ctx", "tp"), None),
            P(("req", "ctx", "tp"), None),
            P("req"),
            P(("req", "ctx"), None),
            P("tp", None),
            P(),
            P(),
            P(None, "tp"),
            P(None, "tp"),
            P("tp", None),
        ),
        out_specs=(P(("req", "ctx", "tp"), None), P(("req", "ctx", "tp"), None)),
        check_vma=False,
    )
```

profile of v0, /device:TPU:0, one launch (start us, length us, event | category | flops | bytes accessed | tf_op | source)
XLA Modules:
  0.0 334.2 jit_solution(5583839891256445070)
XLA Ops:
  12.4 4.8 %collective-permute-done.31 = bf16[128,512]{1,0:T(8,128)(2,1)S(1)} collective-permute-done((bf16[128,512]{1,0:T(8,128)(2,1)}, bf16[128,512]{1,0:T(8,128)(2,1)S(1)}, u32[]{:S(2)}, u32[]{:S(2)}) %collective-permute-start.31) | collective-permute-done | bytes 131104 | tf_op jit(solution)/shard_map/ppermute | solution.py:387
  33.4 4.3 %collective-permute-done.29.refs_4_ = bf16[64,1024]{1,0:T(8,128)(2,1)} collective-permute-done((bf16[64,1024]{1,0:T(8,128)(2,1)}, bf16[64,1024]{1,0:T(8,128)(2,1)}, u32[]{:S(2)}, u32[]{:S(2)}) %collective-permute-start.29) | collective-permute-done | bytes 131104 | tf_op jit(solution)/shard_map/ppermute | solution.py:387
  38.6 6.5 %shard_map.133 = bf16[4,64,1024]{2,1,0:T(8,128)(2,1)S(1)} custom-call(s32[4]{0:T(128)S(1)} %copy-done.4, s32[1]{0:T(128)} %bitcast.8.refs_1_, bf16[64,1024]{1,0:T(8,128)(2,1)S(1)} %collective-permute-done.27.refs_2_, bf16[64,1024]{1,0:T(8,128)(2,1)} %collective-permute-done.28.refs_3_, bf16[64,1024]{1,0:T(8,128)(2,1)} %collective-permute-done.29.refs_4_, ...), custom_call_target="tpu_custom_call" | custom-call | flops 2147483648 | bytes 3145728 | tf_op jit(solution)/shard_map/pallas_call | solution.py:98
  45.0 4.5 %shard_map.134 = bf16[256,3072]{1,0:T(8,128)(2,1)S(1)} custom-call(bf16[256,1024]{1,0:T(8,128)(2,1)S(1)} %bitcast.47, bf16[1024,6144]{1,0:T(8,128)(2,1)} %refs_1_.9, bf16[1024,6144]{1,0:T(8,128)(2,1)} %refs_1_.9), custom_call_target="tpu_custom_call" | custom-call | flops 1610612736 | bytes 6291456 | tf_op jit(solution)/shard_map/pallas_call | solution.py:253
  49.6 4.5 %shard_map.135 = bf16[256,3072]{1,0:T(8,128)(2,1)S(1)} custom-call(bf16[256,1024]{1,0:T(8,128)(2,1)S(1)} %bitcast.48, bf16[1024,6144]{1,0:T(8,128)(2,1)} %refs_1_.9, bf16[1024,6144]{1,0:T(8,128)(2,1)} %refs_1_.9), custom_call_target="tpu_custom_call" | custom-call | flops 1610612736 | bytes 6291456 | tf_op jit(solution)/shard_map/pallas_call | solution.py:253
  61.3 4.5 %collective-permute-start.26 = (bf16[64,1024]{1,0:T(8,128)(2,1)S(1)}, bf16[64,1024]{1,0:T(8,128)(2,1)S(1)}, u32[]{:S(2)}, u32[]{:S(2)}) collective-permute-start(bf16[64,1024]{1,0:T(8,128)(2,1)S(1)} %copy-done.27), channel_id=1, source_target_pairs={{0,3},{1,0},{2,1},{3,2},{4,7},{5,4},{6,5},{7,6},{8,11},{9,8},{10,9... | collective-permute-start | bytes 393224 | tf_op jit(solution)/shard_map/ppermute | solution.py:387
  71.0 15.7 %collective-permute-start.48 = (f32[8,128]{1,0:T(8,128)S(1)}, f32[8,128]{1,0:T(8,128)S(1)}, u32[]{:S(2)}, u32[]{:S(2)}) collective-permute-start(f32[8,128]{1,0:T(8,128)S(1)} %copy-done.23), channel_id=1, source_target_pairs={{0,16},{16,0},{1,17},{17,1},{2,18},{18,2},{3,19},{19,3},{4,20},{20... | collective-permute-start | bytes 12296 | tf_op jit(solution)/shard_map/ppermute | solution.py:565
  94.3 6.3 %shard_map.136 = bf16[4,64,1024]{2,1,0:T(8,128)(2,1)S(1)} custom-call(s32[4]{0:T(128)S(1)} %copy-done.4, s32[1]{0:T(128)} %bitcast.8.refs_1_, bf16[64,1024]{1,0:T(8,128)(2,1)S(1)} %collective-permute-done.24.refs_2_, bf16[64,1024]{1,0:T(8,128)(2,1)S(1)} %collective-permute-done.26.refs_3_, bf16[64,1024]{1,0:T(8,128)(2,1)S(1)} %collective-permute-done.25.refs_4_, ...), custom_call_target="tpu_custom_call" | custom-call | flops 2147483648 | bytes 3145728 | tf_op jit(solution)/shard_map/pallas_call | solution.py:98
  100.6 4.5 %shard_map.137 = bf16[256,3072]{1,0:T(8,128)(2,1)S(1)} custom-call(bf16[256,1024]{1,0:T(8,128)(2,1)S(1)} %bitcast.45, bf16[1024,6144]{1,0:T(8,128)(2,1)} %refs_1_.9, bf16[1024,6144]{1,0:T(8,128)(2,1)} %refs_1_.9), custom_call_target="tpu_custom_call" | custom-call | flops 1610612736 | bytes 6291456 | tf_op jit(solution)/shard_map/pallas_call | solution.py:253
  105.2 7.5 %collective-permute-start.49 = (f32[8,128]{1,0:T(8,128)S(1)}, f32[8,128]{1,0:T(8,128)S(1)}, u32[]{:S(2)}, u32[]{:S(2)}) collective-permute-start(f32[8,128]{1,0:T(8,128)S(1)} %max.9), channel_id=1, source_target_pairs={{0,4},{4,0},{8,12},{12,8},{1,5},{5,1},{9,13},{13,9},{2,6},{6,2},{1... | collective-permute-start | bytes 12296 | tf_op jit(solution)/shard_map/ppermute | solution.py:565
  112.6 4.5 %shard_map.138 = bf16[256,3072]{1,0:T(8,128)(2,1)S(1)} custom-call(bf16[256,1024]{1,0:T(8,128)(2,1)S(1)} %bitcast.46, bf16[1024,6144]{1,0:T(8,128)(2,1)} %refs_1_.9, bf16[1024,6144]{1,0:T(8,128)(2,1)} %refs_1_.9), custom_call_target="tpu_custom_call" | custom-call | flops 1610612736 | bytes 6291456 | tf_op jit(solution)/shard_map/pallas_call | solution.py:253
  117.2 5.0 %collective-permute-start.38 = (bf16[64,3072]{1,0:T(8,128)(2,1)S(1)}, bf16[64,3072]{1,0:T(8,128)(2,1)S(1)}, u32[]{:S(2)}, u32[]{:S(2)}) collective-permute-start(bf16[64,3072]{1,0:T(8,128)(2,1)S(1)} %get-tuple-element.269), channel_id=1, source_target_pairs={{0,1},{1,2},{4,5},{5,6},{8,9},{9,10},{12,13},{13,14},{16,17},{17,1... | collective-permute-start | bytes 1179656 | tf_op jit(solution)/shard_map/ppermute | solution.py:410
  122.9 4.9 %collective-permute-start.46 = (bf16[64,3072]{1,0:T(8,128)(2,1)S(1)}, bf16[64,3072]{1,0:T(8,128)(2,1)S(1)}, u32[]{:S(2)}, u32[]{:S(2)}) collective-permute-start(bf16[64,3072]{1,0:T(8,128)(2,1)S(1)} %get-tuple-element.261), channel_id=1, source_target_pairs={{0,1},{1,2},{2,3},{4,5},{5,6},{6,7},{8,9},{9,10},{10,11},{12,13},{... | collective-permute-start | bytes 1179656 | tf_op jit(solution)/shard_map/ppermute | solution.py:410
  131.7 4.9 %collective-permute-start.40 = (bf16[64,3072]{1,0:T(8,128)(2,1)S(1)}, bf16[64,3072]{1,0:T(8,128)(2,1)S(1)}, u32[]{:S(2)}, u32[]{:S(2)}) collective-permute-start(bf16[64,3072]{1,0:T(8,128)(2,1)S(1)} %get-tuple-element.267), channel_id=1, source_target_pairs={{0,1},{1,2},{2,3},{4,5},{5,6},{6,7},{8,9},{9,10},{10,11},{12,13},{... | collective-permute-start | bytes 1179656 | tf_op jit(solution)/shard_map/ppermute | solution.py:410
  140.1 7.5 %collective-permute-done.40 = bf16[64,3072]{1,0:T(8,128)(2,1)S(1)} collective-permute-done((bf16[64,3072]{1,0:T(8,128)(2,1)S(1)}, bf16[64,3072]{1,0:T(8,128)(2,1)S(1)}, u32[]{:S(2)}, u32[]{:S(2)}) %collective-permute-start.40) | collective-permute-done | bytes 393248 | tf_op jit(solution)/shard_map/ppermute | solution.py:410
  149.9 4.1 %collective-permute-start.51 = (bf16[64,3072]{1,0:T(8,128)(2,1)S(1)}, bf16[64,3072]{1,0:T(8,128)(2,1)S(1)}, u32[]{:S(2)}, u32[]{:S(2)}) collective-permute-start(bf16[64,3072]{1,0:T(8,128)(2,1)S(1)} %get-tuple-element.273.refs_1_), channel_id=1, source_target_pairs={{0,1},{1,2},{2,3},{4,5},{5,6},{6,7},{8,9},{9,10},{10,11},{12,13},{... | collective-permute-start | bytes 1179656 | tf_op jit(solution)/shard_map/ppermute | solution.py:431
  155.4 5.0 %collective-permute-start.57 = (bf16[64,3072]{1,0:T(8,128)(2,1)S(1)}, bf16[64,3072]{1,0:T(8,128)(2,1)S(1)}, u32[]{:S(2)}, u32[]{:S(2)}) collective-permute-start(bf16[64,3072]{1,0:T(8,128)(2,1)S(1)} %get-tuple-element.272.refs_1_), channel_id=1, source_target_pairs={{0,1},{1,2},{2,3},{4,5},{5,6},{6,7},{8,9},{9,10},{10,11},{12,13},{... | collective-permute-start | bytes 1179656 | tf_op jit(solution)/shard_map/ppermute | solution.py:431
  163.6 4.9 %collective-permute-done.52.refs_5_ = bf16[64,3072]{1,0:T(8,128)(2,1)S(1)} collective-permute-done((bf16[64,3072]{1,0:T(8,128)(2,1)S(1)}, bf16[64,3072]{1,0:T(8,128)(2,1)S(1)}, u32[]{:S(2)}, u32[]{:S(2)}) %collective-permute-start.52) | collective-permute-done | bytes 393248 | tf_op jit(solution)/shard_map/ppermute | solution.py:432
  171.0 4.6 %collective-permute-start.53 = (bf16[64,3072]{1,0:T(8,128)(2,1)S(1)}, bf16[64,3072]{1,0:T(8,128)(2,1)S(1)}, u32[]{:S(2)}, u32[]{:S(2)}) collective-permute-start(bf16[64,3072]{1,0:T(8,128)(2,1)S(1)} %add_select_fusion.7), channel_id=1, source_target_pairs={{0,1},{1,2},{2,3},{4,5},{5,6},{6,7},{8,9},{9,10},{10,11},{12,13},{... | collective-permute-start | bytes 1179656 | tf_op jit(solution)/shard_map/ppermute | solution.py:431
  178.5 4.7 %collective-permute-start.59 = (bf16[64,3072]{1,0:T(8,128)(2,1)S(1)}, bf16[64,3072]{1,0:T(8,128)(2,1)S(1)}, u32[]{:S(2)}, u32[]{:S(2)}) collective-permute-start(bf16[64,3072]{1,0:T(8,128)(2,1)S(1)} %add_select_fusion.3), channel_id=1, source_target_pairs={{0,1},{1,2},{2,3},{4,5},{5,6},{6,7},{8,9},{9,10},{10,11},{12,13},{... | collective-permute-start | bytes 1179656 | tf_op jit(solution)/shard_map/ppermute | solution.py:431
  215.3 17.2 %collective-permute-start.64 = (bf16[64,3072]{1,0:T(8,128)(2,1)S(1)}, bf16[64,3072]{1,0:T(8,128)(2,1)S(1)}, u32[]{:S(2)}, u32[]{:S(2)}) collective-permute-start(bf16[64,3072]{1,0:T(8,128)(2,1)S(1)} %add.299), channel_id=1, source_target_pairs={{1,0},{2,1},{3,2},{5,4},{6,5},{7,6},{9,8},{10,9},{11,10},{13,12},{... | collective-permute-start | bytes 1179656 | tf_op jit(solution)/shard_map/ppermute | solution.py:439
  232.5 13.5 %shard_map.139 = (f32[256,2048]{1,0:T(8,128)S(1)}, f32[256,2048]{1,0:T(8,128)S(1)}) custom-call(s32[1]{0:T(128)} %bitcast.6.mine.refs_0_, bf16[64,3072]{1,0:T(8,128)(2,1)S(1)} %get-tuple-element.272.refs_1_, bf16[64,3072]{1,0:T(8,128)(2,1)S(1)} %collective-permute-done.57.refs_2_, bf16[64,3072]{1,0:T(8,128)(2,1)S(1)} %collective-permute-done.59.refs_3_, ...), custom_call_target="tpu_custom_call" | custom-call | flops 6442450944 | bytes 25165824 | tf_op jit(solution)/shard_map/pallas_call | solution.py:203
  246.0 14.3 %shard_map.140.left_ref = bf16[256,2048]{1,0:T(8,128)(2,1)S(1)} custom-call(s32[1]{0:T(128)} %bitcast.6.mine.refs_0_, bf16[64,3072]{1,0:T(8,128)(2,1)S(1)} %get-tuple-element.273.refs_1_, bf16[64,3072]{1,0:T(8,128)(2,1)S(1)} %collective-permute-done.51.refs_2_, bf16[64,3072]{1,0:T(8,128)(2,1)S(1)} %collective-permute-done.53.refs_3_, ...), custom_call_target="tpu_custom_call" | custom-call | flops 6442450944 | bytes 25165824 | tf_op jit(solution)/shard_map/pallas_call | solution.py:203
  260.8 7.9 %shard_map.142 = bf16[256,3072]{1,0:T(8,128)(2,1)S(1)} custom-call(bf16[256,2048]{1,0:T(8,128)(2,1)S(1)} %shard_map.140.left_ref, bf16[2048,6144]{1,0:T(8,128)(2,1)} %refs_1_.11, bf16[2048,6144]{1,0:T(8,128)(2,1)} %refs_1_.11), custom_call_target="tpu_custom_call" | custom-call | flops 3221225472 | bytes 12582912 | tf_op jit(solution)/shard_map/pallas_call | solution.py:253
  268.7 7.9 %shard_map.141 = bf16[256,3072]{1,0:T(8,128)(2,1)S(1)} custom-call(bf16[256,2048]{1,0:T(8,128)(2,1)S(1)} %shard_map.140.left_ref, bf16[2048,6144]{1,0:T(8,128)(2,1)} %refs_1_.11, bf16[2048,6144]{1,0:T(8,128)(2,1)} %refs_1_.11), custom_call_target="tpu_custom_call" | custom-call | flops 3221225472 | bytes 12582912 | tf_op jit(solution)/shard_map/pallas_call | solution.py:253
  276.6 4.6 %collective-permute-start.73 = (bf16[64,3072]{1,0:T(8,128)(2,1)S(1)}, bf16[64,3072]{1,0:T(8,128)(2,1)S(1)}, u32[]{:S(2)}, u32[]{:S(2)}) collective-permute-start(bf16[64,3072]{1,0:T(8,128)(2,1)S(1)} %get-tuple-element.245), channel_id=1, source_target_pairs={{0,1},{4,5},{8,9},{12,13},{16,17},{20,21},{24,25},{28,29}} | collective-permute-start | bytes 1179656 | tf_op jit(solution)/shard_map/ppermute | solution.py:410
  284.0 6.8 %collective-permute-done.73 = bf16[64,3072]{1,0:T(8,128)(2,1)S(1)} collective-permute-done((bf16[64,3072]{1,0:T(8,128)(2,1)S(1)}, bf16[64,3072]{1,0:T(8,128)(2,1)S(1)}, u32[]{:S(2)}, u32[]{:S(2)}) %collective-permute-start.73) | collective-permute-done | bytes 393248 | tf_op jit(solution)/shard_map/ppermute | solution.py:410
  290.8 4.4 %collective-permute-start.75 = (bf16[64,3072]{1,0:T(8,128)(2,1)S(1)}, bf16[64,3072]{1,0:T(8,128)(2,1)S(1)}, u32[]{:S(2)}, u32[]{:S(2)}) collective-permute-start(bf16[64,3072]{1,0:T(8,128)(2,1)S(1)} %get-tuple-element.243), channel_id=1, source_target_pairs={{0,1},{1,2},{4,5},{5,6},{8,9},{9,10},{12,13},{13,14},{16,17},{17,1... | collective-permute-start | bytes 1179656 | tf_op jit(solution)/shard_map/ppermute | solution.py:410
  299.2 4.4 %collective-permute-start.69 = (bf16[64,3072]{1,0:T(8,128)(2,1)S(1)}, bf16[64,3072]{1,0:T(8,128)(2,1)S(1)}, u32[]{:S(2)}, u32[]{:S(2)}) collective-permute-start(bf16[64,3072]{1,0:T(8,128)(2,1)S(1)} %get-tuple-element.237), channel_id=1, source_target_pairs={{0,1},{1,2},{4,5},{5,6},{8,9},{9,10},{12,13},{13,14},{16,17},{17,1... | collective-permute-start | bytes 1179656 | tf_op jit(solution)/shard_map/ppermute | solution.py:410
  307.7 4.5 %collective-permute-start.77 = (bf16[64,3072]{1,0:T(8,128)(2,1)S(1)}, bf16[64,3072]{1,0:T(8,128)(2,1)S(1)}, u32[]{:S(2)}, u32[]{:S(2)}) collective-permute-start(bf16[64,3072]{1,0:T(8,128)(2,1)S(1)} %get-tuple-element.241), channel_id=1, source_target_pairs={{0,1},{1,2},{2,3},{4,5},{5,6},{6,7},{8,9},{9,10},{10,11},{12,13},{... | collective-permute-start | bytes 1179656 | tf_op jit(solution)/shard_map/ppermute | solution.py:410
  316.1 4.4 %collective-permute-start.71 = (bf16[64,3072]{1,0:T(8,128)(2,1)S(1)}, bf16[64,3072]{1,0:T(8,128)(2,1)S(1)}, u32[]{:S(2)}, u32[]{:S(2)}) collective-permute-start(bf16[64,3072]{1,0:T(8,128)(2,1)S(1)} %get-tuple-element.235), channel_id=1, source_target_pairs={{0,1},{1,2},{2,3},{4,5},{5,6},{6,7},{8,9},{9,10},{10,11},{12,13},{... | collective-permute-start | bytes 1179656 | tf_op jit(solution)/shard_map/ppermute | solution.py:410
  326.1 4.1 %collective-permute-done.72 = bf16[64,3072]{1,0:T(8,128)(2,1)S(1)} collective-permute-done((bf16[64,3072]{1,0:T(8,128)(2,1)S(1)}, bf16[64,3072]{1,0:T(8,128)(2,1)S(1)}, u32[]{:S(2)}, u32[]{:S(2)}) %collective-permute-start.72) | collective-permute-done | bytes 393248 | tf_op jit(solution)/shard_map/ppermute | solution.py:411
  (210 shorter events, 124.6 us)
Async XLA Ops:
  17.2 13.8 %collective-permute-start.33 = (bf16[512,512]{1,0:T(8,128)(2,1)S(1)}, bf16[512,512]{1,0:T(8,128)(2,1)S(1)}, u32[]{:S(2)}, u32[]{:S(2)}) collective-permute-start(bf16[512,512]{1,0:T(8,128)(2,1)S(1)} %constant_dynamic-update-slice_fusion.refs_8_), channel_id=1, source_target_pairs={{0,8},{4,12},{8,0},{12,4},{1,9},{5,13},{9,1},{13,5},{2,10},{6,14},... | collective-permute-start | bytes 1572872 | tf_op jit(solution)/shard_map/ppermute | solution.py:473
  56.5 30.2 %collective-permute-start.42 = (bf16[64,3072]{1,0:T(8,128)(2,1)S(1)}, bf16[64,3072]{1,0:T(8,128)(2,1)S(1)}, u32[]{:S(2)}, u32[]{:S(2)}) collective-permute-start(bf16[64,3072]{1,0:T(8,128)(2,1)S(1)} %get-tuple-element.265), channel_id=1, source_target_pairs={{0,1},{4,5},{8,9},{12,13},{16,17},{20,21},{24,25},{28,29}} | collective-permute-start | bytes 1179656 | tf_op jit(solution)/shard_map/ppermute | solution.py:410
  57.8 28.9 %collective-permute-start.43 = (bf16[64,3072]{1,0:T(8,128)(2,1)S(1)}, bf16[64,3072]{1,0:T(8,128)(2,1)S(1)}, u32[]{:S(2)}, u32[]{:S(2)}) collective-permute-start(bf16[64,3072]{1,0:T(8,128)(2,1)S(1)} %get-tuple-element.264), channel_id=1, source_target_pairs={{3,2},{7,6},{11,10},{15,14},{19,18},{23,22},{27,26},{31,30}} | collective-permute-start | bytes 1179656 | tf_op jit(solution)/shard_map/ppermute | solution.py:411
  71.0 34.1 %collective-permute-start.48 = (f32[8,128]{1,0:T(8,128)S(1)}, f32[8,128]{1,0:T(8,128)S(1)}, u32[]{:S(2)}, u32[]{:S(2)}) collective-permute-start(f32[8,128]{1,0:T(8,128)S(1)} %copy-done.23), channel_id=1, source_target_pairs={{0,16},{16,0},{1,17},{17,1},{2,18},{18,2},{3,19},{19,3},{4,20},{20... | collective-permute-start | bytes 12296 | tf_op jit(solution)/shard_map/ppermute | solution.py:565
  86.8 36.0 %collective-permute-start.44 = (bf16[64,3072]{1,0:T(8,128)(2,1)S(1)}, bf16[64,3072]{1,0:T(8,128)(2,1)S(1)}, u32[]{:S(2)}, u32[]{:S(2)}) collective-permute-start(bf16[64,3072]{1,0:T(8,128)(2,1)S(1)} %get-tuple-element.263), channel_id=1, source_target_pairs={{0,1},{1,2},{4,5},{5,6},{8,9},{9,10},{12,13},{13,14},{16,17},{17,1... | collective-permute-start | bytes 1179656 | tf_op jit(solution)/shard_map/ppermute | solution.py:410
  90.5 32.3 %collective-permute-start.45 = (bf16[64,3072]{1,0:T(8,128)(2,1)S(1)}, bf16[64,3072]{1,0:T(8,128)(2,1)S(1)}, u32[]{:S(2)}, u32[]{:S(2)}) collective-permute-start(bf16[64,3072]{1,0:T(8,128)(2,1)S(1)} %get-tuple-element.262), channel_id=1, source_target_pairs={{2,1},{3,2},{6,5},{7,6},{10,9},{11,10},{14,13},{15,14},{18,17},{19... | collective-permute-start | bytes 1179656 | tf_op jit(solution)/shard_map/ppermute | solution.py:411
  91.3 40.4 %collective-permute-start.39 = (bf16[64,3072]{1,0:T(8,128)(2,1)S(1)}, bf16[64,3072]{1,0:T(8,128)(2,1)S(1)}, u32[]{:S(2)}, u32[]{:S(2)}) collective-permute-start(bf16[64,3072]{1,0:T(8,128)(2,1)S(1)} %get-tuple-element.268), channel_id=1, source_target_pairs={{2,1},{3,2},{6,5},{7,6},{10,9},{11,10},{14,13},{15,14},{18,17},{19... | collective-permute-start | bytes 1179656 | tf_op jit(solution)/shard_map/ppermute | solution.py:411
  105.2 17.0 %collective-permute-start.49 = (f32[8,128]{1,0:T(8,128)S(1)}, f32[8,128]{1,0:T(8,128)S(1)}, u32[]{:S(2)}, u32[]{:S(2)}) collective-permute-start(f32[8,128]{1,0:T(8,128)S(1)} %max.9), channel_id=1, source_target_pairs={{0,4},{4,0},{8,12},{12,8},{1,5},{5,1},{9,13},{13,9},{2,6},{6,2},{1... | collective-permute-start | bytes 12296 | tf_op jit(solution)/shard_map/ppermute | solution.py:565
  117.2 14.5 %collective-permute-start.38 = (bf16[64,3072]{1,0:T(8,128)(2,1)S(1)}, bf16[64,3072]{1,0:T(8,128)(2,1)S(1)}, u32[]{:S(2)}, u32[]{:S(2)}) collective-permute-start(bf16[64,3072]{1,0:T(8,128)(2,1)S(1)} %get-tuple-element.269), channel_id=1, source_target_pairs={{0,1},{1,2},{4,5},{5,6},{8,9},{9,10},{12,13},{13,14},{16,17},{17,1... | collective-permute-start | bytes 1179656 | tf_op jit(solution)/shard_map/ppermute | solution.py:410
  122.2 17.0 %collective-permute-start.50 = (f32[8,128]{1,0:T(8,128)S(1)}, f32[8,128]{1,0:T(8,128)S(1)}, u32[]{:S(2)}, u32[]{:S(2)}) collective-permute-start(f32[8,128]{1,0:T(8,128)S(1)} %max.10), channel_id=1, source_target_pairs={{0,8},{4,12},{8,0},{12,4},{1,9},{5,13},{9,1},{13,5},{2,10},{6,14},... | collective-permute-start | bytes 12296 | tf_op jit(solution)/shard_map/ppermute | solution.py:565
  122.9 17.2 %collective-permute-start.46 = (bf16[64,3072]{1,0:T(8,128)(2,1)S(1)}, bf16[64,3072]{1,0:T(8,128)(2,1)S(1)}, u32[]{:S(2)}, u32[]{:S(2)}) collective-permute-start(bf16[64,3072]{1,0:T(8,128)(2,1)S(1)} %get-tuple-element.261), channel_id=1, source_target_pairs={{0,1},{1,2},{2,3},{4,5},{5,6},{6,7},{8,9},{9,10},{10,11},{12,13},{... | collective-permute-start | bytes 1179656 | tf_op jit(solution)/shard_map/ppermute | solution.py:410
  131.7 15.8 %collective-permute-start.40 = (bf16[64,3072]{1,0:T(8,128)(2,1)S(1)}, bf16[64,3072]{1,0:T(8,128)(2,1)S(1)}, u32[]{:S(2)}, u32[]{:S(2)}) collective-permute-start(bf16[64,3072]{1,0:T(8,128)(2,1)S(1)} %get-tuple-element.267), channel_id=1, source_target_pairs={{0,1},{1,2},{2,3},{4,5},{5,6},{6,7},{8,9},{9,10},{10,11},{12,13},{... | collective-permute-start | bytes 1179656 | tf_op jit(solution)/shard_map/ppermute | solution.py:410
  149.9 13.7 %collective-permute-start.51 = (bf16[64,3072]{1,0:T(8,128)(2,1)S(1)}, bf16[64,3072]{1,0:T(8,128)(2,1)S(1)}, u32[]{:S(2)}, u32[]{:S(2)}) collective-permute-start(bf16[64,3072]{1,0:T(8,128)(2,1)S(1)} %get-tuple-element.273.refs_1_), channel_id=1, source_target_pairs={{0,1},{1,2},{2,3},{4,5},{5,6},{6,7},{8,9},{9,10},{10,11},{12,13},{... | collective-permute-start | bytes 1179656 | tf_op jit(solution)/shard_map/ppermute | solution.py:431
  154.1 14.4 %collective-permute-start.52 = (bf16[64,3072]{1,0:T(8,128)(2,1)S(1)}, bf16[64,3072]{1,0:T(8,128)(2,1)S(1)}, u32[]{:S(2)}, u32[]{:S(2)}) collective-permute-start(bf16[64,3072]{1,0:T(8,128)(2,1)S(1)} %get-tuple-element.273.refs_1_), channel_id=1, source_target_pairs={{1,0},{2,1},{3,2},{5,4},{6,5},{7,6},{9,8},{10,9},{11,10},{13,12},{... | collective-permute-start | bytes 1179656 | tf_op jit(solution)/shard_map/ppermute | solution.py:432
  155.4 20.2 %collective-permute-start.57 = (bf16[64,3072]{1,0:T(8,128)(2,1)S(1)}, bf16[64,3072]{1,0:T(8,128)(2,1)S(1)}, u32[]{:S(2)}, u32[]{:S(2)}) collective-permute-start(bf16[64,3072]{1,0:T(8,128)(2,1)S(1)} %get-tuple-element.272.refs_1_), channel_id=1, source_target_pairs={{0,1},{1,2},{2,3},{4,5},{5,6},{6,7},{8,9},{9,10},{10,11},{12,13},{... | collective-permute-start | bytes 1179656 | tf_op jit(solution)/shard_map/ppermute | solution.py:431
  160.4 16.5 %collective-permute-start.58 = (bf16[64,3072]{1,0:T(8,128)(2,1)S(1)}, bf16[64,3072]{1,0:T(8,128)(2,1)S(1)}, u32[]{:S(2)}, u32[]{:S(2)}) collective-permute-start(bf16[64,3072]{1,0:T(8,128)(2,1)S(1)} %get-tuple-element.272.refs_1_), channel_id=1, source_target_pairs={{1,0},{2,1},{3,2},{5,4},{6,5},{7,6},{9,8},{10,9},{11,10},{13,12},{... | collective-permute-start | bytes 1179656 | tf_op jit(solution)/shard_map/ppermute | solution.py:432
  169.5 15.8 %collective-permute-start.54 = (bf16[64,3072]{1,0:T(8,128)(2,1)S(1)}, bf16[64,3072]{1,0:T(8,128)(2,1)S(1)}, u32[]{:S(2)}, u32[]{:S(2)}) collective-permute-start(bf16[64,3072]{1,0:T(8,128)(2,1)S(1)} %add_select_fusion.6), channel_id=1, source_target_pairs={{1,0},{2,1},{3,2},{5,4},{6,5},{7,6},{9,8},{10,9},{11,10},{13,12},{... | collective-permute-start | bytes 1179656 | tf_op jit(solution)/shard_map/ppermute | solution.py:432
  171.0 14.3 %collective-permute-start.53 = (bf16[64,3072]{1,0:T(8,128)(2,1)S(1)}, bf16[64,3072]{1,0:T(8,128)(2,1)S(1)}, u32[]{:S(2)}, u32[]{:S(2)}) collective-permute-start(bf16[64,3072]{1,0:T(8,128)(2,1)S(1)} %add_select_fusion.7), channel_id=1, source_target_pairs={{0,1},{1,2},{2,3},{4,5},{5,6},{6,7},{8,9},{9,10},{10,11},{12,13},{... | collective-permute-start | bytes 1179656 | tf_op jit(solution)/shard_map/ppermute | solution.py:431
  176.9 16.8 %collective-permute-start.60 = (bf16[64,3072]{1,0:T(8,128)(2,1)S(1)}, bf16[64,3072]{1,0:T(8,128)(2,1)S(1)}, u32[]{:S(2)}, u32[]{:S(2)}) collective-permute-start(bf16[64,3072]{1,0:T(8,128)(2,1)S(1)} %add_select_fusion.2), channel_id=1, source_target_pairs={{1,0},{2,1},{3,2},{5,4},{6,5},{7,6},{9,8},{10,9},{11,10},{13,12},{... | collective-permute-start | bytes 1179656 | tf_op jit(solution)/shard_map/ppermute | solution.py:432
  178.5 15.3 %collective-permute-start.59 = (bf16[64,3072]{1,0:T(8,128)(2,1)S(1)}, bf16[64,3072]{1,0:T(8,128)(2,1)S(1)}, u32[]{:S(2)}, u32[]{:S(2)}) collective-permute-start(bf16[64,3072]{1,0:T(8,128)(2,1)S(1)} %add_select_fusion.3), channel_id=1, source_target_pairs={{0,1},{1,2},{2,3},{4,5},{5,6},{6,7},{8,9},{9,10},{10,11},{12,13},{... | collective-permute-start | bytes 1179656 | tf_op jit(solution)/shard_map/ppermute | solution.py:431
  185.4 15.7 %collective-permute-start.55 = (bf16[64,3072]{1,0:T(8,128)(2,1)S(1)}, bf16[64,3072]{1,0:T(8,128)(2,1)S(1)}, u32[]{:S(2)}, u32[]{:S(2)}) collective-permute-start(bf16[64,3072]{1,0:T(8,128)(2,1)S(1)} %get-tuple-element.277), channel_id=1, source_target_pairs={{0,1},{1,2},{2,3},{4,5},{5,6},{6,7},{8,9},{9,10},{10,11},{12,13},{... | collective-permute-start | bytes 1179656 | tf_op jit(solution)/shard_map/ppermute | solution.py:431
  193.8 15.7 %collective-permute-start.61 = (bf16[64,3072]{1,0:T(8,128)(2,1)S(1)}, bf16[64,3072]{1,0:T(8,128)(2,1)S(1)}, u32[]{:S(2)}, u32[]{:S(2)}) collective-permute-start(bf16[64,3072]{1,0:T(8,128)(2,1)S(1)} %get-tuple-element.275), channel_id=1, source_target_pairs={{0,1},{1,2},{2,3},{4,5},{5,6},{6,7},{8,9},{9,10},{10,11},{12,13},{... | collective-permute-start | bytes 1179656 | tf_op jit(solution)/shard_map/ppermute | solution.py:431
  202.8 57.5 %collective-permute-start.65 = (bf16[64,3072]{1,0:T(8,128)(2,1)S(1)}, bf16[64,3072]{1,0:T(8,128)(2,1)S(1)}, u32[]{:S(2)}, u32[]{:S(2)}) collective-permute-start(bf16[64,3072]{1,0:T(8,128)(2,1)S(1)} %add.302), channel_id=1, source_target_pairs={{0,1},{1,2},{2,3},{4,5},{5,6},{6,7},{8,9},{9,10},{10,11},{12,13},{... | collective-permute-start | bytes 1179656 | tf_op jit(solution)/shard_map/ppermute | solution.py:438
  206.3 54.0 %collective-permute-start.66 = (bf16[64,3072]{1,0:T(8,128)(2,1)S(1)}, bf16[64,3072]{1,0:T(8,128)(2,1)S(1)}, u32[]{:S(2)}, u32[]{:S(2)}) collective-permute-start(bf16[64,3072]{1,0:T(8,128)(2,1)S(1)} %add.304), channel_id=1, source_target_pairs={{1,0},{2,1},{3,2},{5,4},{6,5},{7,6},{9,8},{10,9},{11,10},{13,12},{... | collective-permute-start | bytes 1179656 | tf_op jit(solution)/shard_map/ppermute | solution.py:439
  211.1 49.2 %collective-permute-start.63 = (bf16[64,3072]{1,0:T(8,128)(2,1)S(1)}, bf16[64,3072]{1,0:T(8,128)(2,1)S(1)}, u32[]{:S(2)}, u32[]{:S(2)}) collective-permute-start(bf16[64,3072]{1,0:T(8,128)(2,1)S(1)} %add.297), channel_id=1, source_target_pairs={{0,1},{1,2},{2,3},{4,5},{5,6},{6,7},{8,9},{9,10},{10,11},{12,13},{... | collective-permute-start | bytes 1179656 | tf_op jit(solution)/shard_map/ppermute | solution.py:438
  215.3 45.1 %collective-permute-start.64 = (bf16[64,3072]{1,0:T(8,128)(2,1)S(1)}, bf16[64,3072]{1,0:T(8,128)(2,1)S(1)}, u32[]{:S(2)}, u32[]{:S(2)}) collective-permute-start(bf16[64,3072]{1,0:T(8,128)(2,1)S(1)} %add.299), channel_id=1, source_target_pairs={{1,0},{2,1},{3,2},{5,4},{6,5},{7,6},{9,8},{10,9},{11,10},{13,12},{... | collective-permute-start | bytes 1179656 | tf_op jit(solution)/shard_map/ppermute | solution.py:439
  276.6 14.1 %collective-permute-start.73 = (bf16[64,3072]{1,0:T(8,128)(2,1)S(1)}, bf16[64,3072]{1,0:T(8,128)(2,1)S(1)}, u32[]{:S(2)}, u32[]{:S(2)}) collective-permute-start(bf16[64,3072]{1,0:T(8,128)(2,1)S(1)} %get-tuple-element.245), channel_id=1, source_target_pairs={{0,1},{4,5},{8,9},{12,13},{16,17},{20,21},{24,25},{28,29}} | collective-permute-start | bytes 1179656 | tf_op jit(solution)/shard_map/ppermute | solution.py:410
  282.0 17.2 %collective-permute-start.67 = (bf16[64,3072]{1,0:T(8,128)(2,1)S(1)}, bf16[64,3072]{1,0:T(8,128)(2,1)S(1)}, u32[]{:S(2)}, u32[]{:S(2)}) collective-permute-start(bf16[64,3072]{1,0:T(8,128)(2,1)S(1)} %get-tuple-element.239), channel_id=1, source_target_pairs={{0,1},{4,5},{8,9},{12,13},{16,17},{20,21},{24,25},{28,29}} | collective-permute-start | bytes 1179656 | tf_op jit(solution)/shard_map/ppermute | solution.py:410
  283.3 15.9 %collective-permute-start.68 = (bf16[64,3072]{1,0:T(8,128)(2,1)S(1)}, bf16[64,3072]{1,0:T(8,128)(2,1)S(1)}, u32[]{:S(2)}, u32[]{:S(2)}) collective-permute-start(bf16[64,3072]{1,0:T(8,128)(2,1)S(1)} %get-tuple-element.238), channel_id=1, source_target_pairs={{3,2},{7,6},{11,10},{15,14},{19,18},{23,22},{27,26},{31,30}} | collective-permute-start | bytes 1179656 | tf_op jit(solution)/shard_map/ppermute | solution.py:411
  290.8 16.8 %collective-permute-start.75 = (bf16[64,3072]{1,0:T(8,128)(2,1)S(1)}, bf16[64,3072]{1,0:T(8,128)(2,1)S(1)}, u32[]{:S(2)}, u32[]{:S(2)}) collective-permute-start(bf16[64,3072]{1,0:T(8,128)(2,1)S(1)} %get-tuple-element.243), channel_id=1, source_target_pairs={{0,1},{1,2},{4,5},{5,6},{8,9},{9,10},{12,13},{13,14},{16,17},{17,1... | collective-permute-start | bytes 1179656 | tf_op jit(solution)/shard_map/ppermute | solution.py:410
  299.2 16.8 %collective-permute-start.69 = (bf16[64,3072]{1,0:T(8,128)(2,1)S(1)}, bf16[64,3072]{1,0:T(8,128)(2,1)S(1)}, u32[]{:S(2)}, u32[]{:S(2)}) collective-permute-start(bf16[64,3072]{1,0:T(8,128)(2,1)S(1)} %get-tuple-element.237), channel_id=1, source_target_pairs={{0,1},{1,2},{4,5},{5,6},{8,9},{9,10},{12,13},{13,14},{16,17},{17,1... | collective-permute-start | bytes 1179656 | tf_op jit(solution)/shard_map/ppermute | solution.py:410
  307.7 15.9 %collective-permute-start.77 = (bf16[64,3072]{1,0:T(8,128)(2,1)S(1)}, bf16[64,3072]{1,0:T(8,128)(2,1)S(1)}, u32[]{:S(2)}, u32[]{:S(2)}) collective-permute-start(bf16[64,3072]{1,0:T(8,128)(2,1)S(1)} %get-tuple-element.241), channel_id=1, source_target_pairs={{0,1},{1,2},{2,3},{4,5},{5,6},{6,7},{8,9},{9,10},{10,11},{12,13},{... | collective-permute-start | bytes 1179656 | tf_op jit(solution)/shard_map/ppermute | solution.py:410
  (53 other events, 648.2 us)
where the time goes:
time: 337 us; the launch traced here: 334 us
  starting transfers between devices  158 us (47%)
  Pallas kernels  79.1 us (23%)
  waiting for transfers between devices  75 us (22%)
  local copies, waits for them, and re-layouts  7.66 us (2%)
  other arithmetic  7.02 us (2%)
  matrix products  4.49 us (1%)
    ppermute x12, starting transfers between devices, reduce_line(): right = lax.ppermute(to_right, 'tp', rights(s))  45 us
    pallas_call x6, Pallas kernels, product(): pl.pallas_call(functools.partial(product_kernel, streams), grid=(steps,),...  33.9 us
    ppermute x12, waiting for transfers between devices, reduce_line(): right = lax.ppermute(to_right, 'tp', rights(s))  31.4 us
    pallas_call x2, Pallas kernels, hidden_units(): pl.pallas_call(functools.partial(hidden_kernel, len(sources), len(before)...  27.8 us
    ppermute x6, starting transfers between devices, gather_line(): right = lax.ppermute(right, 'tp', to_right)  26.5 us
    ppermute x3, starting transfers between devices, on_device(): lax.ppermute(fullest, axis, [(i, i ^ step) for i in range(size)])  23.7 us
    ppermute x2, starting transfers between devices, gather_line(): left = lax.ppermute(left + terms[1], 'tp', lefts(shards - 1))  18.5 us
    ppermute x9, starting transfers between devices, shift(): lax.ppermute(parts[s], 'tp', moves[s])  16.8 us
  transfers between devices with their start and end apart: 55, of which 26 were waited for; matrix products, arithmetic and copies ran while one was open for 4% of the time, Pallas kernels for 14%

commit v1 on v0

--- a/solution.py
+++ b/solution.py
@@ -17,7 +17,7 @@
 TILE = 256
 
 
-def attention_kernel(slots, held, pairs, sharing, block_rows, *refs):
+def attention_kernel(slots, together, held, pairs, sharing, block_rows, *refs):
     (order, mine), refs = refs[:2], refs[2:]
     query_refs, refs = refs[:slots], refs[slots:]
     place_ref, key_place_ref, refs = refs[0], refs[1], refs[2:]
@@ -42,12 +42,13 @@
 
     for at in range(slots):
 
-        @pl.when(pl.program_id(0) == at)
+        @pl.when(pl.program_id(0) == at // together)
         def _():
             for p in range(pairs):
                 for g in range(sharing):
                     column = (p * sharing + g) * HD
-                    query_ref[p, g * half : (g + 1) * half, :] = query_refs[at][:, column : column + HD]
+                    row = (at % together * sharing + g) * half
+                    query_ref[p, row : row + half, :] = query_refs[at][:, column : column + HD]
 
     def scores_of(p, at):
         ref, index, _ = blocks[at]
@@ -59,7 +60,7 @@
     def mixed_of(p, at, weights):
         return jnp.dot(value_ref[at, p], weights, preferred_element_type=jnp.float32)
 
-    place = jnp.concatenate([place_ref[0]] * sharing, axis=1)
+    place = jnp.concatenate([place_ref[i] for i in range(together) for _ in range(sharing)], axis=1)
     visible = key_place_ref[...] <= place
     for p in range(pairs):
         scores = jnp.where(visible, scores_of(p, 0), -1e30)
@@ -82,31 +83,34 @@
 
     for p in range(pairs):
         mixed = (total_ref[p, :HD, :] / total_ref[p, HD : HD + 1, :]).T.astype(jnp.bfloat16)
-        for g in range(sharing):
-            column = (p * sharing + g) * HD
-            out_ref[0, :, column : column + HD] = mixed[g * half : (g + 1) * half]
+        for i in range(together):
+            for g in range(sharing):
+                column = (p * sharing + g) * HD
+                row = (i * sharing + g) * half
+                out_ref[i, :, column : column + HD] = mixed[row : row + half]
 
 
 def attend(order, mine, queries, places, key_places, pair_list, held, pairs, sharing, block_rows):
     slots = len(queries)
     half, width = queries[0].shape
-    tall = sharing * half
+    together = 2 if slots <= LINE else 1
+    tall = together * sharing * half
     blocks = sum(len(group) for group in held)
     count = blocks * block_rows
-    kernel = functools.partial(attention_kernel, slots, held, pairs, sharing, block_rows)
+    kernel = functools.partial(attention_kernel, slots, together, held, pairs, sharing, block_rows)
     whole = [pl.BlockSpec(pair.shape, lambda s, *_: (0, 0)) for pair in pair_list]
     return pl.pallas_call(
         kernel,
         grid_spec=pltpu.PrefetchScalarGridSpec(
             num_scalar_prefetch=2,
-            grid=(slots,),
+            grid=(slots // together,),
             in_specs=[pl.BlockSpec((half, width), lambda s, *_: (0, 0))] * slots
             + [
-                pl.BlockSpec((1, 1, half), lambda s, *_: (s, 0, 0)),
+                pl.BlockSpec((together, 1, half), lambda s, *_: (s, 0, 0)),
                 pl.BlockSpec((block_rows, 1), lambda s, *_: (0, 0)),
             ]
             + whole,
-            out_specs=pl.BlockSpec((1, half, width), lambda s, *_: (s, 0, 0)),
+            out_specs=pl.BlockSpec((together, half, width), lambda s, *_: (s, 0, 0)),
             scratch_shapes=[
                 pltpu.VMEM((pairs, tall, HD), jnp.bfloat16),
                 pltpu.VMEM((blocks, pairs, HD + SUM_ROWS, block_rows), jnp.bfloat16),
@@ -115,19 +119,19 @@
             ],
         ),
         out_shape=jax.ShapeDtypeStruct((slots, half, width), jnp.bfloat16),
-        compiler_params=pltpu.CompilerParams(vmem_limit_bytes=24 * 1024 * 1024),
+        compiler_params=pltpu.CompilerParams(vmem_limit_bytes=12 * 1024 * 1024),
         cost_estimate=pl.CostEstimate(
-            flops=4 * slots * half * width * count,
+            flops=40 * slots * half * width * count,
             bytes_accessed=2 * (2 * slots * half * width + count * 2 * pairs * HD),
             transcendentals=slots * half * width // HD * count,
         ),
     )(order, mine, *queries, places, key_places, *pair_list)
 
 
-def hidden_kernel(plan, started, last, streams, *refs):
+def hidden_kernel(plan, started, last, cut, *refs):
     mine, refs = refs[0], refs[1:]
     sources, refs = refs[:plan], refs[plan:]
-    gate_weights, up_weights, refs = refs[:streams], refs[streams : 2 * streams], refs[2 * streams :]
+    gate_weight, up_weight, refs = refs[0], refs[1], refs[2:]
     if started:
         gate_before, up_before, refs = refs[0], refs[1], refs[2:]
     if last:
@@ -136,35 +140,37 @@
         gate, upward, chosen = refs
     step = pl.program_id(0)
     steps = pl.num_programs(0)
-    tile = gate_weights[0].shape[0]
+    tile = up_weight.shape[0]
+    depth = chosen.shape[1]
+
+    def piece(ref):
+        return ref[...] if ref.shape[1] == depth else ref[:, cut * depth : (cut + 1) * depth]
 
     @pl.when(step == 0)
     def _():
-        if plan == 1:
-            chosen[...] = sources[0][...]
-        else:
-            shards = (plan + 1) // 2
-            rows = sources[0].shape[0]
-            chosen[:rows] = sources[0][...]
-            for s in range(1, shards):
-                right, left = sources[s], sources[plan - s]
-
-                @pl.when(mine[0] >= s)
-                def _():
-                    chosen[s * rows : (s + 1) * rows] = right[...]
-
-                @pl.when(mine[0] < s)
-                def _():
-                    chosen[s * rows : (s + 1) * rows] = left[...]
-
-    parts = []
-    for weights in (gate_weights, up_weights):
-        total = None
-        for j, weight in enumerate(weights):
-            columns = pl.ds(pl.multiple_of((j * steps + step) * tile, tile), tile)
-            term = jnp.dot(chosen[:, columns], weight[...], preferred_element_type=jnp.float32)
-            total = term if total is None else total + term
-        parts.append(total)
+        shards = (plan + 1) // 2
+        rows = sources[0].shape[0]
+        chosen[:rows] = piece(sources[0])
+        for s in range(1, shards):
+            right, left = sources[s], sources[plan - s]
+
+            @pl.when(mine[0] >= s)
+            def _():
+                chosen[s * rows : (s + 1) * rows] = piece(right)
+
+            @pl.when(mine[0] < s)
+            def _():
+                chosen[s * rows : (s + 1) * rows] = piece(left)
+
+    held = chosen[:, pl.ds(pl.multiple_of(step * tile, tile), tile)]
+    if gate_weight.shape[0] == tile:
+        gate_tile = gate_weight[...]
+    else:
+        gate_tile = gate_weight[pl.ds(pl.multiple_of((cut * steps + step) * tile, tile), tile), :]
+    parts = [
+        jnp.dot(held, gate_tile, preferred_element_type=jnp.float32),
+        jnp.dot(held, up_weight[...], preferred_element_type=jnp.float32),
+    ]
 
     @pl.when(step == 0)
     def _():
@@ -184,52 +190,45 @@
             out[...] = (value / (1.0 + jnp.exp(-value)) * upward[...]).astype(jnp.bfloat16)
 
 
-def hidden_units(mine, sources, gate_weight, up_weight, cut, before, last):
+def hidden_units(mine, sources, gate_weight, up_weight, cut, pieces, before, resident):
     shards = (len(sources) + 1) // 2
     rows = sources[0].shape[0] * shards
-    depth = sources[0].shape[1]
+    depth = gate_weight.shape[0] // pieces
     width = gate_weight.shape[1]
-    tile, streams = TILE, 2
-    steps = depth // (tile * streams)
-    weights = [
-        pl.BlockSpec((tile, width), functools.partial(lambda j, k, *_: ((cut * streams + j) * steps + k, 0), j))
-        for j in range(streams)
-    ]
-    out = pl.BlockSpec((rows, width), lambda k, *_: (0, 0))
+    last = cut == pieces - 1
+    tile = TILE
+    steps = depth // tile
+    streamed = pl.BlockSpec((tile, width), lambda k, *_: (cut * steps + k, 0))
+    in_place = pl.BlockSpec(memory_space=pltpu.VMEM)
+    out = pl.BlockSpec(memory_space=pltpu.VMEM)
     kinds = [jnp.bfloat16] if last else [jnp.float32] * 2
     scratch = [pltpu.VMEM((rows, depth), jnp.bfloat16)]
     if last:
         scratch += [pltpu.VMEM((rows, width), jnp.float32)] * 2
     return pl.pallas_call(
-        functools.partial(hidden_kernel, len(sources), len(before) > 0, last, streams),
+        functools.partial(hidden_kernel, len(sources), len(before) > 0, last, cut),
         grid_spec=pltpu.PrefetchScalarGridSpec(
             num_scalar_prefetch=1,
             grid=(steps,),
-            in_specs=[pl.BlockSpec(source.shape, lambda k, *_: (0, 0)) for source in sources]
-            + weights
-            + weights
-            + [out] * len(before),
+            in_specs=[in_place] * len(sources)
+            + [in_place if resident else streamed, streamed]
+            + [in_place] * len(before),
             out_specs=[out] * len(kinds),
             scratch_shapes=scratch,
         ),
         out_shape=[jax.ShapeDtypeStruct((rows, width), kind) for kind in kinds],
-        compiler_params=pltpu.CompilerParams(vmem_limit_bytes=40 * 1024 * 1024),
+        compiler_params=pltpu.CompilerParams(vmem_limit_bytes=24 * 1024 * 1024),
         cost_estimate=pl.CostEstimate(
             flops=4 * rows * depth * width, bytes_accessed=4 * depth * width, transcendentals=rows * width
         ),
-    )(mine, *sources, *[gate_weight] * streams, *[up_weight] * streams, *before)
-
-
-def product_kernel(streams, left_ref, *refs):
-    weights, (out_ref, total) = refs[:streams], refs[streams:]
+    )(mine, *sources, gate_weight, up_weight, *before)
+
+
+def product_kernel(left_ref, weight, out_ref, total):
     step = pl.program_id(0)
-    steps = pl.num_programs(0)
-    tile = weights[0].shape[0]
-    value = None
-    for j, weight in enumerate(weights):
-        columns = pl.ds(pl.multiple_of((j * steps + step) * tile, tile), tile)
-        term = jnp.dot(left_ref[:, columns], weight[...], preferred_element_type=jnp.float32)
-        value = term if value is None else value + term
+    tile = weight.shape[0]
+    columns = pl.ds(pl.multiple_of(step * tile, tile), tile)
+    value = jnp.dot(left_ref[:, columns], weight[...], preferred_element_type=jnp.float32)
 
     @pl.when(step == 0)
     def _():
@@ -239,33 +238,50 @@
     def _():
         total[...] += value
 
-    @pl.when(step == steps - 1)
+    @pl.when(step == pl.num_programs(0) - 1)
     def _():
         out_ref[...] = total[...].astype(jnp.bfloat16)
 
 
-def product(left, weight, cut, pieces):
+def resident_product_kernel(cut, left_ref, weight, out_ref):
+    tile = out_ref.shape[1]
+    columns = pl.ds(pl.multiple_of((cut * pl.num_programs(0) + pl.program_id(0)) * tile, tile), tile)
+    out_ref[...] = jnp.dot(left_ref[...], weight[:, columns], preferred_element_type=jnp.float32).astype(
+        jnp.bfloat16
+    )
+
+
+def product(left, weight, cut, pieces, resident=False):
     rows, depth = left.shape
     width = weight.shape[1] // pieces
+    cost = pl.CostEstimate(flops=2 * rows * depth * width, bytes_accessed=2 * depth * width, transcendentals=0)
+    out = jax.ShapeDtypeStruct((rows, width), jnp.bfloat16)
+    limit = pltpu.CompilerParams(vmem_limit_bytes=20 * 1024 * 1024)
+    if resident:
+        tile = 1024
+        return pl.pallas_call(
+            functools.partial(resident_product_kernel, cut),
+            grid=(width // tile,),
+            in_specs=[pl.BlockSpec((rows, depth), lambda n: (0, 0)), pl.BlockSpec(memory_space=pltpu.VMEM)],
+            out_specs=pl.BlockSpec((rows, tile), lambda n: (0, n)),
+            out_shape=out,
+            compiler_params=limit,
+            cost_estimate=cost,
+        )(left, weight)
     tile = min(TILE, depth)
-    streams = 2 if depth % (2 * tile) == 0 else 1
-    steps = depth // (tile * streams)
     return pl.pallas_call(
-        functools.partial(product_kernel, streams),
-        grid=(steps,),
-        in_specs=[pl.BlockSpec((rows, depth), lambda k: (0, 0))]
-        + [
-            pl.BlockSpec((tile, width), functools.partial(lambda j, k: (j * steps + k, cut), j))
-            for j in range(streams)
+        product_kernel,
+        grid=(depth // tile,),
+        in_specs=[
+            pl.BlockSpec((rows, depth), lambda k: (0, 0)),
+            pl.BlockSpec((tile, width), lambda k: (k, cut)),
         ],
         out_specs=pl.BlockSpec((rows, width), lambda k: (0, 0)),
-        out_shape=jax.ShapeDtypeStruct((rows, width), jnp.bfloat16),
+        out_shape=out,
         scratch_shapes=[pltpu.VMEM((rows, width), jnp.float32)],
-        compiler_params=pltpu.CompilerParams(vmem_limit_bytes=40 * 1024 * 1024),
-        cost_estimate=pl.CostEstimate(
-            flops=2 * rows * depth * width, bytes_accessed=2 * depth * width, transcendentals=0
-        ),
-    )(left, *[weight] * streams)
+        compiler_params=limit,
+        cost_estimate=cost,
+    )(left, weight)
 
 
 def pack_pairs_kernel(shards, mine, keys_ref, values_ref, *outs):
@@ -401,7 +417,8 @@
         if not line:
             by_shard = jnp.take(jnp.stack(terms), shard_of, axis=0).reshape(-1, terms[0].shape[1])
             return lax.psum_scatter(by_shard, "tp", scatter_dimension=0, tiled=True).astype(jnp.float32), None
-        right = left = mark = None
+        right = left = None
+        marks = []
         for s in range(1, shards):
             to_right, to_left = terms[s], terms[shards - s]
             if right is not None:
@@ -410,35 +427,41 @@
             right = lax.ppermute(to_right, "tp", rights(s))
             left = lax.ppermute(to_left, "tp", lefts(s))
             right, left = lax.optimization_barrier((right, left))
-            mark = right if mark is None else mark
-        return terms[0].astype(jnp.float32) + right.astype(jnp.float32) + left.astype(jnp.float32), mark
+            marks.append(right)
+        return terms[0].astype(jnp.float32) + right.astype(jnp.float32) + left.astype(jnp.float32), marks
 
     def gather_line(source, terms=None):
         if not line:
             got = lax.all_gather(source, "tp", axis=0)
-            return [jnp.take(got, shard_of, axis=0).reshape(shards * half, -1)], None
-        right = left = source
-        from_left, from_right = [], []
-        for s in range(1, shards):
-            if s > 1 and terms is not None:
-                right = jnp.where(me >= s - 1, right, right + terms[s - 1])
-                left = jnp.where(me <= shards - s, left, left + terms[shards - s + 1])
-            if s == 1 or terms is not None:
-                to_right, to_left = rights(shards - 1), lefts(shards - 1)
-            else:
-                to_right = [(i, i + 1) for i in range(s - 1, shards - 1)]
-                to_left = [(i, i - 1) for i in range(1, shards - s + 1)]
-            right = lax.ppermute(right, "tp", to_right)
-            left = lax.ppermute(left, "tp", to_left)
-            right, left = lax.optimization_barrier((right, left))
-            from_left.append(right)
-            from_right.append(left)
-        total = None
-        if terms is not None:
-            right = lax.ppermute(right + terms[shards - 1], "tp", rights(shards - 1))
-            left = lax.ppermute(left + terms[1], "tp", lefts(shards - 1))
-            total = terms[0].astype(jnp.float32) + right.astype(jnp.float32) + left.astype(jnp.float32)
-        return [source] + from_left + from_right, total
+            return [[jnp.take(got, shard_of, axis=0).reshape(shards * half, -1)]], None
+        first_right = lax.ppermute(source, "tp", rights(shards - 1))
+        first_left = lax.ppermute(source, "tp", lefts(shards - 1))
+        first_right, first_left = lax.optimization_barrier((first_right, first_left))
+        sources, totals = [], []
+        for c, cut in enumerate(cuts):
+            right, left = first_right[:, cut], first_left[:, cut]
+            from_left, from_right = [first_right], [first_left]
+            for s in range(2, shards):
+                if terms is None:
+                    to_right = [(i, i + 1) for i in range(s - 1, shards - 1)]
+                    to_left = [(i, i - 1) for i in range(1, shards - s + 1)]
+                else:
+                    right = jnp.where(me >= s - 1, right, right + terms[c][s - 1])
+                    left = jnp.where(me <= shards - s, left, left + terms[c][shards - s + 1])
+                    to_right, to_left = rights(shards - 1), lefts(shards - 1)
+                right = lax.ppermute(right, "tp", to_right)
+                left = lax.ppermute(left, "tp", to_left)
+                right, left = lax.optimization_barrier((right, left))
+                from_left.append(right)
+                from_right.append(left)
+            if terms is not None:
+                right = lax.ppermute(right + terms[c][shards - 1], "tp", rights(shards - 1))
+                left = lax.ppermute(left + terms[c][1], "tp", lefts(shards - 1))
+                totals.append(
+                    terms[c][0].astype(jnp.float32) + right.astype(jnp.float32) + left.astype(jnp.float32)
+                )
+            sources.append([source] + from_left + from_right)
+        return sources, totals
 
     key_places = (shard_of[:, None] * rows + jnp.arange(rows, dtype=jnp.int32)[None, :]).reshape(block_rows, 1)
     picked = ((routes[:, 0] == 0) | (routes[:, 1] == 0)).reshape(shards, rows)
@@ -512,18 +535,18 @@
             [(base[:, cut] + head_sum).astype(jnp.bfloat16) for cut, head_sum in zip(cuts, head_sums)], axis=1
         )
 
-    def activate(attended, terms=None):
+    def normalise(attended):
         widened = attended.astype(jnp.float32)
-        normed = (
+        return (
             widened * lax.rsqrt(jnp.mean(widened * widened, axis=1, keepdims=True) + 1e-05) * norm_gain
         ).astype(jnp.bfloat16)
+
+    def activate(normed, terms=None, resident=False):
+        sources, sums = gather_line(normed, terms)
         before = []
-        sums = []
-        for c, cut in enumerate(cuts):
-            sources, total = gather_line(normed[:, cut], None if terms is None else terms[c])
-            sums.append(total)
-            before = hidden_units(me[None], sources, gate_weight, up_weight, c, before, c == pieces - 1)
-        return normed, before[0], sums
+        for c in range(pieces):
+            before = hidden_units(me[None], sources[c], gate_weight, up_weight, c, pieces, before, resident)
+        return before[0], sums
 
     def share_of(which, normed):
         logits = jnp.dot(normed, router_weight, preferred_element_type=jnp.float32)
@@ -542,33 +565,28 @@
         return jnp.concatenate(parts, axis=1)
 
     def late_expert(source):
-        normed, acts, _ = activate(source)
+        normed = normalise(source)
+        acts, _ = activate(normed, None, False)
         return deliver(acts, share_of(1, normed))
 
-    reduced = [reduce_line(terms) for terms in project(0)]
+    terms = project(0)
+    if halves > 1:
+        terms, asked[1] = lax.optimization_barrier((terms, asked[1]))
+    reduced = [reduce_line(term) for term in terms]
     if line:
-        asked[-1], hidden_in, order, fullest, _ = lax.optimization_barrier(
-            (asked[-1], hidden_in, order, fullest, reduced[0][1])
-        )
+        hidden_in, order, _ = lax.optimization_barrier((hidden_in, order, reduced[0][1][0]))
     hidden = reorder(hidden_in)
     my_routes = lax.dynamic_slice_in_dim(routes, me * rows, rows, 0).astype(jnp.bfloat16)
     my_routes = reorder(my_routes).astype(jnp.int32)
     totals = [total for total, _ in reduced]
+    first_half = finish(0, totals)
+    normed = normalise(first_half)
+    share = share_of(0, normed)
     if halves == 1:
-        first_half = finish(0, totals)
-        normed, acts, _ = activate(first_half)
-        return (restore([first_half]), restore([deliver(acts, share_of(0, normed))]))
-    for axis in ("req", "ctx"):
-        size = lax.axis_size(axis)
-        step = 1
-        while step < size:
-            fullest = jnp.maximum(fullest, lax.ppermute(fullest, axis, [(i, i ^ step) for i in range(size)]))
-            step *= 2
-    terms = project(1)
-    totals, terms, fullest = lax.optimization_barrier((totals, terms, fullest))
-    first_half = finish(0, totals)
-    normed, acts, sums = activate(first_half, terms)
-    share = share_of(0, normed)
+        acts, _ = activate(normed)
+        return (restore([first_half]), restore([deliver(acts, share)]))
+    asked[1], _ = lax.optimization_barrier((asked[1], normed))
+    acts, sums = activate(normed, project(1))
     second_half = finish(1, sums)
     acts, second_half = lax.optimization_barrier((acts, second_half))
     part = deliver(acts, share)

time: 337 us -> 333 us (0.988)
  the two profiles are of different devices: /device:TPU:0 before, /device:TPU:12 now
where the time goes in v1:
time: 333 us
  starting transfers between devices  125 us (38%)
  Pallas kernels  91.6 us (28%)
  waiting for transfers between devices  81.2 us (24%)
  local copies, waits for them, and re-layouts  16.2 us (5%)
  other arithmetic  12.4 us (4%)
  matrix products  4.51 us (1%)
    ppermute x12, starting transfers between devices, reduce_line(): right = lax.ppermute(to_right, 'tp', rights(s))  39.3 us
    pallas_call x6, Pallas kernels, product(): pl.pallas_call(product_kernel, grid=(depth // tile,), in_specs=[pl.BlockS...  36.9 us
    ppermute x12, waiting for transfers between devices, reduce_line(): right = lax.ppermute(to_right, 'tp', rights(s))  36.7 us
    pallas_call x2, Pallas kernels, hidden_units(): pl.pallas_call(functools.partial(hidden_kernel, len(sources), len(before)...  36.1 us
    ppermute x2, starting transfers between devices, gather_line(): left = lax.ppermute(left + terms[c][1], 'tp', lefts(shards - 1))  18.4 us
    ppermute x12, starting transfers between devices, reduce_line(): left = lax.ppermute(to_left, 'tp', lefts(s))  16.7 us
    ppermute x4, starting transfers between devices, gather_line(): right = lax.ppermute(right, 'tp', to_right)  15.6 us
    pallas_call x2, Pallas kernels, attend(): pl.pallas_call(kernel, grid_spec=pltpu.PrefetchScalarGridSpec(num_scalar_...  13.9 us
  transfers between devices with their start and end apart: 50, of which 26 were waited for; matrix products, arithmetic and copies ran while one was open for 5% of the time, Pallas kernels for 21%

profile of v1, /device:TPU:12, one launch (start us, length us, event | category | flops | bytes accessed | tf_op | source)
XLA Modules:
  0.0 333.5 jit_solution(3772513467113797604)
XLA Ops:
  8.2 5.9 %collective-permute-done.25 = bf16[128,512]{1,0:T(8,128)(2,1)S(1)} collective-permute-done((bf16[128,512]{1,0:T(8,128)(2,1)}, bf16[128,512]{1,0:T(8,128)(2,1)S(1)}, u32[]{:S(2)}, u32[]{:S(2)}) %collective-permute-start.25) | collective-permute-done | bytes 131104 | tf_op jit(solution)/shard_map/ppermute | solution.py:403
  26.0 5.3 %collective-permute-done.28.refs_9_ = bf16[512,512]{1,0:T(8,128)(2,1)S(1)} collective-permute-done((bf16[512,512]{1,0:T(8,128)(2,1)S(1)}, bf16[512,512]{1,0:T(8,128)(2,1)S(1)}, u32[]{:S(2)}, u32[]{:S(2)}) %collective-permute-start.28) | collective-permute-done | bytes 524320 | tf_op jit(solution)/shard_map/ppermute | solution.py:496
  38.9 7.0 %shard_map.133 = bf16[4,64,1024]{2,1,0:T(8,128)(2,1)S(1)} custom-call(s32[4]{0:T(128)S(1)} %copy-done.19, s32[1]{0:T(128)} %bitcast.8.refs_1_, bf16[64,1024]{1,0:T(8,128)(2,1)S(1)} %copy-done.18, bf16[64,1024]{1,0:T(8,128)(2,1)} %collective-permute-done.23.refs_3_, bf16[64,1024]{1,0:T(8,128)(2,1)} %collective-permute-done.24.refs_4_, ...), custom_call_target="tpu_custom_call" | custom-call | flops 21474836480 | bytes 3145728 | tf_op jit(solution)/shard_map/pallas_call | solution.py:102
  46.0 4.6 %copy-done.2 = bf16[1024,6144]{1,0:T(8,128)(2,1)S(1)} copy-done((bf16[1024,6144]{1,0:T(8,128)(2,1)S(1)}, bf16[1024,6144]{1,0:T(8,128)(2,1)}, u32[]{:S(2)}) %copy-start.2) | copy-done | bytes 12582936
  50.6 4.0 %shard_map.135 = bf16[256,3072]{1,0:T(8,128)(2,1)S(1)} custom-call(bf16[256,1024]{1,0:T(8,128)(2,1)S(1)} %bitcast.49, bf16[1024,6144]{1,0:T(8,128)(2,1)S(1)} %copy-done.2), custom_call_target="tpu_custom_call" | custom-call | flops 1610612736 | bytes 6291456 | tf_op jit(solution)/shard_map/pallas_call | solution.py:272
  54.6 4.0 %shard_map.134 = bf16[256,3072]{1,0:T(8,128)(2,1)S(1)} custom-call(bf16[256,1024]{1,0:T(8,128)(2,1)S(1)} %bitcast.50, bf16[1024,6144]{1,0:T(8,128)(2,1)S(1)} %copy-done.2), custom_call_target="tpu_custom_call" | custom-call | flops 1610612736 | bytes 6291456 | tf_op jit(solution)/shard_map/pallas_call | solution.py:272
  66.2 8.3 %collective-permute-done.34 = bf16[64,3072]{1,0:T(8,128)(2,1)} collective-permute-done((bf16[64,3072]{1,0:T(8,128)(2,1)}, bf16[64,3072]{1,0:T(8,128)(2,1)}, u32[]{:S(2)}, u32[]{:S(2)}) %collective-permute-start.34) | collective-permute-done | bytes 393248 | tf_op jit(solution)/shard_map/ppermute | solution.py:427
  77.1 4.6 %collective-permute-start.36 = (bf16[64,3072]{1,0:T(8,128)(2,1)S(1)}, bf16[64,3072]{1,0:T(8,128)(2,1)S(1)}, u32[]{:S(2)}, u32[]{:S(2)}) collective-permute-start(bf16[64,3072]{1,0:T(8,128)(2,1)S(1)} %get-tuple-element.271), channel_id=1, source_target_pairs={{0,1},{1,2},{4,5},{5,6},{8,9},{9,10},{12,13},{13,14},{16,17},{17,1... | collective-permute-start | bytes 1179656 | tf_op jit(solution)/shard_map/ppermute | solution.py:427
  84.2 4.6 %collective-permute-start.42 = (bf16[64,3072]{1,0:T(8,128)(2,1)S(1)}, bf16[64,3072]{1,0:T(8,128)(2,1)S(1)}, u32[]{:S(2)}, u32[]{:S(2)}) collective-permute-start(bf16[64,3072]{1,0:T(8,128)(2,1)S(1)} %get-tuple-element.273), channel_id=1, source_target_pairs={{0,1},{1,2},{4,5},{5,6},{8,9},{9,10},{12,13},{13,14},{16,17},{17,1... | collective-permute-start | bytes 1179656 | tf_op jit(solution)/shard_map/ppermute | solution.py:427
  95.4 3.9 %collective-permute-start.38 = (bf16[64,3072]{1,0:T(8,128)(2,1)S(1)}, bf16[64,3072]{1,0:T(8,128)(2,1)S(1)}, u32[]{:S(2)}, u32[]{:S(2)}) collective-permute-start(bf16[64,3072]{1,0:T(8,128)(2,1)S(1)} %add.276), channel_id=1, source_target_pairs={{0,1},{1,2},{2,3},{4,5},{5,6},{6,7},{8,9},{9,10},{10,11},{12,13},{... | collective-permute-start | bytes 1179656 | tf_op jit(solution)/shard_map/ppermute | solution.py:427
  102.0 4.2 %collective-permute-start.44 = (bf16[64,3072]{1,0:T(8,128)(2,1)S(1)}, bf16[64,3072]{1,0:T(8,128)(2,1)S(1)}, u32[]{:S(2)}, u32[]{:S(2)}) collective-permute-start(bf16[64,3072]{1,0:T(8,128)(2,1)S(1)} %add.283), channel_id=1, source_target_pairs={{0,1},{1,2},{2,3},{4,5},{5,6},{6,7},{8,9},{9,10},{10,11},{12,13},{... | collective-permute-start | bytes 1179656 | tf_op jit(solution)/shard_map/ppermute | solution.py:427
  108.0 6.0 %collective-permute-done.45 = bf16[64,3072]{1,0:T(8,128)(2,1)S(1)} collective-permute-done((bf16[64,3072]{1,0:T(8,128)(2,1)S(1)}, bf16[64,3072]{1,0:T(8,128)(2,1)S(1)}, u32[]{:S(2)}, u32[]{:S(2)}) %collective-permute-start.45) | collective-permute-done | bytes 393248 | tf_op jit(solution)/shard_map/ppermute | solution.py:428
  120.4 4.2 %collective-permute-start.46 = (bf16[64,6144]{1,0:T(8,128)(2,1)S(1)}, bf16[64,6144]{1,0:T(8,128)(2,1)S(1)}, u32[]{:S(2)}, u32[]{:S(2)}) collective-permute-start(bf16[64,6144]{1,0:T(8,128)(2,1)S(1)} %fusion.7.refs_1_), channel_id=1, source_target_pairs={{0,1},{1,2},{2,3},{4,5},{5,6},{6,7},{8,9},{9,10},{10,11},{12,13},{... | collective-permute-start | bytes 2359304 | tf_op jit(solution)/shard_map/ppermute | solution.py:437
  124.7 6.9 %shard_map.136 = bf16[4,64,1024]{2,1,0:T(8,128)(2,1)S(1)} custom-call(s32[4]{0:T(128)S(1)} %copy-done.19, s32[1]{0:T(128)} %bitcast.8.refs_1_, bf16[64,1024]{1,0:T(8,128)(2,1)S(1)} %collective-permute-done.31.refs_2_, bf16[64,1024]{1,0:T(8,128)(2,1)S(1)} %copy-done.15, bf16[64,1024]{1,0:T(8,128)(2,1)S(1)} %copy-done.13, bf16[64,1024]{1,0:T(8,128)(2,1)S(1)} %copy-done.11, ...), custom_call_target="tpu_custom_call" | custom-call | flops 21474836480 | bytes 3145728 | tf_op jit(solution)/shard_map/pallas_call | solution.py:102
  131.6 4.0 %shard_map.138 = bf16[256,3072]{1,0:T(8,128)(2,1)S(1)} custom-call(bf16[256,1024]{1,0:T(8,128)(2,1)S(1)} %bitcast.47, bf16[1024,6144]{1,0:T(8,128)(2,1)S(1)} %bitcast.46), custom_call_target="tpu_custom_call" | custom-call | flops 1610612736 | bytes 6291456 | tf_op jit(solution)/shard_map/pallas_call | solution.py:272
  135.7 4.0 %shard_map.137 = bf16[256,3072]{1,0:T(8,128)(2,1)S(1)} custom-call(bf16[256,1024]{1,0:T(8,128)(2,1)S(1)} %bitcast.48, bf16[1024,6144]{1,0:T(8,128)(2,1)S(1)} %bitcast.46), custom_call_target="tpu_custom_call" | custom-call | flops 1610612736 | bytes 6291456 | tf_op jit(solution)/shard_map/pallas_call | solution.py:272
  146.3 3.9 %collective-permute-start.48 = (bf16[64,3072]{1,0:T(8,128)(2,1)}, bf16[64,3072]{1,0:T(8,128)(2,1)}, u32[]{:S(2)}, u32[]{:S(2)}) collective-permute-start(bf16[64,3072]{1,0:T(8,128)(2,1)} %get-tuple-element.257), channel_id=1, source_target_pairs={{0,1},{1,2},{2,3},{4,5},{5,6},{6,7},{8,9},{9,10},{10,11},{12,13},{... | collective-permute-start | bytes 1179656 | tf_op jit(solution)/shard_map/ppermute | solution.py:452
  150.2 3.9 %collective-permute-start.52 = (bf16[64,3072]{1,0:T(8,128)(2,1)}, bf16[64,3072]{1,0:T(8,128)(2,1)}, u32[]{:S(2)}, u32[]{:S(2)}) collective-permute-start(bf16[64,3072]{1,0:T(8,128)(2,1)} %get-tuple-element.258), channel_id=1, source_target_pairs={{0,1},{1,2},{2,3},{4,5},{5,6},{6,7},{8,9},{9,10},{10,11},{12,13},{... | collective-permute-start | bytes 1179656 | tf_op jit(solution)/shard_map/ppermute | solution.py:452
  160.4 8.0 %collective-permute-done.52.refs_3_ = bf16[64,3072]{1,0:T(8,128)(2,1)} collective-permute-done((bf16[64,3072]{1,0:T(8,128)(2,1)}, bf16[64,3072]{1,0:T(8,128)(2,1)}, u32[]{:S(2)}, u32[]{:S(2)}) %collective-permute-start.52) | collective-permute-done | bytes 393248 | tf_op jit(solution)/shard_map/ppermute | solution.py:452
  171.5 3.9 %collective-permute-start.54 = (bf16[64,3072]{1,0:T(8,128)(2,1)S(1)}, bf16[64,3072]{1,0:T(8,128)(2,1)S(1)}, u32[]{:S(2)}, u32[]{:S(2)}) collective-permute-start(bf16[64,3072]{1,0:T(8,128)(2,1)S(1)} %get-tuple-element.251), channel_id=1, source_target_pairs={{0,1},{1,2},{2,3},{4,5},{5,6},{6,7},{8,9},{9,10},{10,11},{12,13},{... | collective-permute-start | bytes 1179656 | tf_op jit(solution)/shard_map/ppermute | solution.py:452
  178.5 3.9 %collective-permute-start.50 = (bf16[64,3072]{1,0:T(8,128)(2,1)S(1)}, bf16[64,3072]{1,0:T(8,128)(2,1)S(1)}, u32[]{:S(2)}, u32[]{:S(2)}) collective-permute-start(bf16[64,3072]{1,0:T(8,128)(2,1)S(1)} %get-tuple-element.255), channel_id=1, source_target_pairs={{0,1},{1,2},{2,3},{4,5},{5,6},{6,7},{8,9},{9,10},{10,11},{12,13},{... | collective-permute-start | bytes 1179656 | tf_op jit(solution)/shard_map/ppermute | solution.py:452
  185.4 5.2 %collective-permute-done.51.refs_7_ = bf16[64,3072]{1,0:T(8,128)(2,1)S(1)} collective-permute-done((bf16[64,3072]{1,0:T(8,128)(2,1)S(1)}, bf16[64,3072]{1,0:T(8,128)(2,1)S(1)}, u32[]{:S(2)}, u32[]{:S(2)}) %collective-permute-start.51) | collective-permute-done | bytes 393248 | tf_op jit(solution)/shard_map/ppermute | solution.py:453
  202.4 16.2 %collective-permute-start.57 = (bf16[64,3072]{1,0:T(8,128)(2,1)S(1)}, bf16[64,3072]{1,0:T(8,128)(2,1)S(1)}, u32[]{:S(2)}, u32[]{:S(2)}) collective-permute-start(bf16[64,3072]{1,0:T(8,128)(2,1)S(1)} %get-tuple-element.245), channel_id=1, source_target_pairs={{1,0},{2,1},{3,2},{5,4},{6,5},{7,6},{9,8},{10,9},{11,10},{13,12},{... | collective-permute-start | bytes 1179656 | tf_op jit(solution)/shard_map/ppermute | solution.py:459
  218.6 17.6 %shard_map.139 = (f32[256,2048]{1,0:T(8,128)S(1)}, f32[256,2048]{1,0:T(8,128)S(1)}) custom-call(s32[1]{0:T(128)} %bitcast.6.mine.refs_0_, bf16[64,6144]{1,0:T(8,128)(2,1)S(1)} %fusion.7.refs_1_, bf16[64,6144]{1,0:T(8,128)(2,1)S(1)} %copy-done.6, bf16[64,3072]{1,0:T(8,128)(2,1)} %collective-permute-done.52.refs_3_, ...), custom_call_target="tpu_custom_call" | custom-call | flops 6442450944 | bytes 25165824 | tf_op jit(solution)/shard_map/pallas_call | solution.py:208
  236.2 18.5 %shard_map.140.left_ref = bf16[256,2048]{1,0:T(8,128)(2,1)S(1)} custom-call(s32[1]{0:T(128)} %bitcast.6.mine.refs_0_, bf16[64,6144]{1,0:T(8,128)(2,1)S(1)} %fusion.7.refs_1_, bf16[64,6144]{1,0:T(8,128)(2,1)S(1)} %copy-done.6, bf16[64,3072]{1,0:T(8,128)(2,1)} %collective-permute-done.48.refs_3_, bf16[64,3072]{1,0:T(8,128)(2,1)S(1)} %collective-permute-done.50.refs_4_, ...), custom_call_target="tpu_custom_call" | custom-call | flops 6442450944 | bytes 25165824 | tf_op jit(solution)/shard_map/pallas_call | solution.py:208
  255.2 10.4 %shard_map.142 = bf16[256,3072]{1,0:T(8,128)(2,1)S(1)} custom-call(bf16[256,2048]{1,0:T(8,128)(2,1)S(1)} %shard_map.140.left_ref, bf16[2048,6144]{1,0:T(8,128)(2,1)} %weight.11), custom_call_target="tpu_custom_call" | custom-call | flops 3221225472 | bytes 12582912 | tf_op jit(solution)/shard_map/pallas_call | solution.py:272
  265.6 10.4 %shard_map.141 = bf16[256,3072]{1,0:T(8,128)(2,1)S(1)} custom-call(bf16[256,2048]{1,0:T(8,128)(2,1)S(1)} %shard_map.140.left_ref, bf16[2048,6144]{1,0:T(8,128)(2,1)} %weight.11), custom_call_target="tpu_custom_call" | custom-call | flops 3221225472 | bytes 12582912 | tf_op jit(solution)/shard_map/pallas_call | solution.py:272
  280.2 10.6 %collective-permute-done.60 = bf16[64,3072]{1,0:T(8,128)(2,1)S(1)} collective-permute-done((bf16[64,3072]{1,0:T(8,128)(2,1)S(1)}, bf16[64,3072]{1,0:T(8,128)(2,1)S(1)}, u32[]{:S(2)}, u32[]{:S(2)}) %collective-permute-start.60) | collective-permute-done | bytes 393248 | tf_op jit(solution)/shard_map/ppermute | solution.py:427
  292.1 4.6 %collective-permute-start.62 = (bf16[64,3072]{1,0:T(8,128)(2,1)S(1)}, bf16[64,3072]{1,0:T(8,128)(2,1)S(1)}, u32[]{:S(2)}, u32[]{:S(2)}) collective-permute-start(bf16[64,3072]{1,0:T(8,128)(2,1)S(1)} %get-tuple-element.233), channel_id=1, source_target_pairs={{0,1},{1,2},{4,5},{5,6},{8,9},{9,10},{12,13},{13,14},{16,17},{17,1... | collective-permute-start | bytes 1179656 | tf_op jit(solution)/shard_map/ppermute | solution.py:427
  300.5 4.6 %collective-permute-start.68 = (bf16[64,3072]{1,0:T(8,128)(2,1)S(1)}, bf16[64,3072]{1,0:T(8,128)(2,1)S(1)}, u32[]{:S(2)}, u32[]{:S(2)}) collective-permute-start(bf16[64,3072]{1,0:T(8,128)(2,1)S(1)} %get-tuple-element.239), channel_id=1, source_target_pairs={{0,1},{1,2},{4,5},{5,6},{8,9},{9,10},{12,13},{13,14},{16,17},{17,1... | collective-permute-start | bytes 1179656 | tf_op jit(solution)/shard_map/ppermute | solution.py:427
  309.8 3.9 %collective-permute-start.64 = (bf16[64,3072]{1,0:T(8,128)(2,1)S(1)}, bf16[64,3072]{1,0:T(8,128)(2,1)S(1)}, u32[]{:S(2)}, u32[]{:S(2)}) collective-permute-start(bf16[64,3072]{1,0:T(8,128)(2,1)S(1)} %get-tuple-element.231), channel_id=1, source_target_pairs={{0,1},{1,2},{2,3},{4,5},{5,6},{6,7},{8,9},{9,10},{10,11},{12,13},{... | collective-permute-start | bytes 1179656 | tf_op jit(solution)/shard_map/ppermute | solution.py:427
  318.1 3.9 %collective-permute-start.70 = (bf16[64,3072]{1,0:T(8,128)(2,1)S(1)}, bf16[64,3072]{1,0:T(8,128)(2,1)S(1)}, u32[]{:S(2)}, u32[]{:S(2)}) collective-permute-start(bf16[64,3072]{1,0:T(8,128)(2,1)S(1)} %get-tuple-element.237), channel_id=1, source_target_pairs={{0,1},{1,2},{2,3},{4,5},{5,6},{6,7},{8,9},{9,10},{10,11},{12,13},{... | collective-permute-start | bytes 1179656 | tf_op jit(solution)/shard_map/ppermute | solution.py:427
  (214 shorter events, 120.1 us)
Async XLA Ops:
  34.3 25.8 %collective-permute-start.31 = (bf16[64,1024]{1,0:T(8,128)(2,1)}, bf16[64,1024]{1,0:T(8,128)(2,1)S(1)}, u32[]{:S(2)}, u32[]{:S(2)}) collective-permute-start(bf16[64,1024]{1,0:T(8,128)(2,1)} %get-tuple-element.144), channel_id=1, source_target_pairs={{0,1},{1,2},{2,3},{3,0},{4,5},{5,6},{6,7},{7,4},{8,9},{9,10},{10,1... | collective-permute-start | bytes 393224 | tf_op jit(solution)/shard_map/ppermute | solution.py:403
  34.3 25.8 %collective-permute-start.32 = (bf16[64,1024]{1,0:T(8,128)(2,1)}, bf16[64,1024]{1,0:T(8,128)(2,1)S(1)}, u32[]{:S(2)}, u32[]{:S(2)}) collective-permute-start(bf16[64,1024]{1,0:T(8,128)(2,1)} %get-tuple-element.145), channel_id=1, source_target_pairs={{0,2},{1,3},{2,0},{3,1},{4,6},{5,7},{6,4},{7,5},{8,10},{9,11},{10,... | collective-permute-start | bytes 393224 | tf_op jit(solution)/shard_map/ppermute | solution.py:403
  35.3 25.4 %collective-permute-start.33 = (bf16[64,1024]{1,0:T(8,128)(2,1)}, bf16[64,1024]{1,0:T(8,128)(2,1)S(1)}, u32[]{:S(2)}, u32[]{:S(2)}) collective-permute-start(bf16[64,1024]{1,0:T(8,128)(2,1)} %get-tuple-element.146), channel_id=1, source_target_pairs={{0,3},{1,0},{2,1},{3,2},{4,7},{5,4},{6,5},{7,6},{8,11},{9,8},{10,9... | collective-permute-start | bytes 393224 | tf_op jit(solution)/shard_map/ppermute | solution.py:403
  64.1 17.6 %collective-permute-start.41 = (bf16[64,3072]{1,0:T(8,128)(2,1)S(1)}, bf16[64,3072]{1,0:T(8,128)(2,1)S(1)}, u32[]{:S(2)}, u32[]{:S(2)}) collective-permute-start(bf16[64,3072]{1,0:T(8,128)(2,1)S(1)} %get-tuple-element.160), channel_id=1, source_target_pairs={{3,2},{7,6},{11,10},{15,14},{19,18},{23,22},{27,26},{31,30}} | collective-permute-start | bytes 1179656 | tf_op jit(solution)/shard_map/ppermute | solution.py:428
  64.9 17.9 %collective-permute-start.40 = (bf16[64,3072]{1,0:T(8,128)(2,1)S(1)}, bf16[64,3072]{1,0:T(8,128)(2,1)S(1)}, u32[]{:S(2)}, u32[]{:S(2)}) collective-permute-start(bf16[64,3072]{1,0:T(8,128)(2,1)S(1)} %get-tuple-element.162), channel_id=1, source_target_pairs={{0,1},{4,5},{8,9},{12,13},{16,17},{20,21},{24,25},{28,29}} | collective-permute-start | bytes 1179656 | tf_op jit(solution)/shard_map/ppermute | solution.py:427
  77.1 14.1 %collective-permute-start.36 = (bf16[64,3072]{1,0:T(8,128)(2,1)S(1)}, bf16[64,3072]{1,0:T(8,128)(2,1)S(1)}, u32[]{:S(2)}, u32[]{:S(2)}) collective-permute-start(bf16[64,3072]{1,0:T(8,128)(2,1)S(1)} %get-tuple-element.271), channel_id=1, source_target_pairs={{0,1},{1,2},{4,5},{5,6},{8,9},{9,10},{12,13},{13,14},{16,17},{17,1... | collective-permute-start | bytes 1179656 | tf_op jit(solution)/shard_map/ppermute | solution.py:427
  82.9 16.4 %collective-permute-start.43 = (bf16[64,3072]{1,0:T(8,128)(2,1)S(1)}, bf16[64,3072]{1,0:T(8,128)(2,1)S(1)}, u32[]{:S(2)}, u32[]{:S(2)}) collective-permute-start(bf16[64,3072]{1,0:T(8,128)(2,1)S(1)} %get-tuple-element.272), channel_id=1, source_target_pairs={{2,1},{3,2},{6,5},{7,6},{10,9},{11,10},{14,13},{15,14},{18,17},{19... | collective-permute-start | bytes 1179656 | tf_op jit(solution)/shard_map/ppermute | solution.py:428
  84.2 15.5 %collective-permute-start.42 = (bf16[64,3072]{1,0:T(8,128)(2,1)S(1)}, bf16[64,3072]{1,0:T(8,128)(2,1)S(1)}, u32[]{:S(2)}, u32[]{:S(2)}) collective-permute-start(bf16[64,3072]{1,0:T(8,128)(2,1)S(1)} %get-tuple-element.273), channel_id=1, source_target_pairs={{0,1},{1,2},{4,5},{5,6},{8,9},{9,10},{12,13},{13,14},{16,17},{17,1... | collective-permute-start | bytes 1179656 | tf_op jit(solution)/shard_map/ppermute | solution.py:427
  93.4 14.1 %collective-permute-start.39 = (bf16[64,3072]{1,0:T(8,128)(2,1)S(1)}, bf16[64,3072]{1,0:T(8,128)(2,1)S(1)}, u32[]{:S(2)}, u32[]{:S(2)}) collective-permute-start(bf16[64,3072]{1,0:T(8,128)(2,1)S(1)} %add.277), channel_id=1, source_target_pairs={{1,0},{2,1},{3,2},{5,4},{6,5},{7,6},{9,8},{10,9},{11,10},{13,12},{... | collective-permute-start | bytes 1179656 | tf_op jit(solution)/shard_map/ppermute | solution.py:428
  99.9 14.1 %collective-permute-start.45 = (bf16[64,3072]{1,0:T(8,128)(2,1)S(1)}, bf16[64,3072]{1,0:T(8,128)(2,1)S(1)}, u32[]{:S(2)}, u32[]{:S(2)}) collective-permute-start(bf16[64,3072]{1,0:T(8,128)(2,1)S(1)} %add.284), channel_id=1, source_target_pairs={{1,0},{2,1},{3,2},{5,4},{6,5},{7,6},{9,8},{10,9},{11,10},{13,12},{... | collective-permute-start | bytes 1179656 | tf_op jit(solution)/shard_map/ppermute | solution.py:428
  102.0 14.5 %collective-permute-start.44 = (bf16[64,3072]{1,0:T(8,128)(2,1)S(1)}, bf16[64,3072]{1,0:T(8,128)(2,1)S(1)}, u32[]{:S(2)}, u32[]{:S(2)}) collective-permute-start(bf16[64,3072]{1,0:T(8,128)(2,1)S(1)} %add.283), channel_id=1, source_target_pairs={{0,1},{1,2},{2,3},{4,5},{5,6},{6,7},{8,9},{9,10},{10,11},{12,13},{... | collective-permute-start | bytes 1179656 | tf_op jit(solution)/shard_map/ppermute | solution.py:427
  118.1 22.4 %collective-permute-start.47 = (bf16[64,6144]{1,0:T(8,128)(2,1)S(1)}, bf16[64,6144]{1,0:T(8,128)(2,1)S(1)}, u32[]{:S(2)}, u32[]{:S(2)}) collective-permute-start(bf16[64,6144]{1,0:T(8,128)(2,1)S(1)} %fusion.7.refs_1_), channel_id=1, source_target_pairs={{1,0},{2,1},{3,2},{5,4},{6,5},{7,6},{9,8},{10,9},{11,10},{13,12},{... | collective-permute-start | bytes 2359304 | tf_op jit(solution)/shard_map/ppermute | solution.py:438
  120.4 22.5 %collective-permute-start.46 = (bf16[64,6144]{1,0:T(8,128)(2,1)S(1)}, bf16[64,6144]{1,0:T(8,128)(2,1)S(1)}, u32[]{:S(2)}, u32[]{:S(2)}) collective-permute-start(bf16[64,6144]{1,0:T(8,128)(2,1)S(1)} %fusion.7.refs_1_), channel_id=1, source_target_pairs={{0,1},{1,2},{2,3},{4,5},{5,6},{6,7},{8,9},{9,10},{10,11},{12,13},{... | collective-permute-start | bytes 2359304 | tf_op jit(solution)/shard_map/ppermute | solution.py:437
  144.4 14.4 %collective-permute-start.49 = (bf16[64,3072]{1,0:T(8,128)(2,1)}, bf16[64,3072]{1,0:T(8,128)(2,1)S(1)}, u32[]{:S(2)}, u32[]{:S(2)}) collective-permute-start(bf16[64,3072]{1,0:T(8,128)(2,1)} %get-tuple-element.256), channel_id=1, source_target_pairs={{1,0},{2,1},{3,2},{5,4},{6,5},{7,6},{9,8},{10,9},{11,10},{13,12},{... | collective-permute-start | bytes 1179656 | tf_op jit(solution)/shard_map/ppermute | solution.py:453
  146.3 14.1 %collective-permute-start.48 = (bf16[64,3072]{1,0:T(8,128)(2,1)}, bf16[64,3072]{1,0:T(8,128)(2,1)}, u32[]{:S(2)}, u32[]{:S(2)}) collective-permute-start(bf16[64,3072]{1,0:T(8,128)(2,1)} %get-tuple-element.257), channel_id=1, source_target_pairs={{0,1},{1,2},{2,3},{4,5},{5,6},{6,7},{8,9},{9,10},{10,11},{12,13},{... | collective-permute-start | bytes 1179656 | tf_op jit(solution)/shard_map/ppermute | solution.py:452
  150.2 18.2 %collective-permute-start.52 = (bf16[64,3072]{1,0:T(8,128)(2,1)}, bf16[64,3072]{1,0:T(8,128)(2,1)}, u32[]{:S(2)}, u32[]{:S(2)}) collective-permute-start(bf16[64,3072]{1,0:T(8,128)(2,1)} %get-tuple-element.258), channel_id=1, source_target_pairs={{0,1},{1,2},{2,3},{4,5},{5,6},{6,7},{8,9},{9,10},{10,11},{12,13},{... | collective-permute-start | bytes 1179656 | tf_op jit(solution)/shard_map/ppermute | solution.py:452
  154.1 14.3 %collective-permute-start.53 = (bf16[64,3072]{1,0:T(8,128)(2,1)}, bf16[64,3072]{1,0:T(8,128)(2,1)}, u32[]{:S(2)}, u32[]{:S(2)}) collective-permute-start(bf16[64,3072]{1,0:T(8,128)(2,1)} %get-tuple-element.259), channel_id=1, source_target_pairs={{1,0},{2,1},{3,2},{5,4},{6,5},{7,6},{9,8},{10,9},{11,10},{13,12},{... | collective-permute-start | bytes 1179656 | tf_op jit(solution)/shard_map/ppermute | solution.py:453
  176.5 14.1 %collective-permute-start.51 = (bf16[64,3072]{1,0:T(8,128)(2,1)S(1)}, bf16[64,3072]{1,0:T(8,128)(2,1)S(1)}, u32[]{:S(2)}, u32[]{:S(2)}) collective-permute-start(bf16[64,3072]{1,0:T(8,128)(2,1)S(1)} %get-tuple-element.254), channel_id=1, source_target_pairs={{1,0},{2,1},{3,2},{5,4},{6,5},{7,6},{9,8},{10,9},{11,10},{13,12},{... | collective-permute-start | bytes 1179656 | tf_op jit(solution)/shard_map/ppermute | solution.py:453
  178.5 14.1 %collective-permute-start.50 = (bf16[64,3072]{1,0:T(8,128)(2,1)S(1)}, bf16[64,3072]{1,0:T(8,128)(2,1)S(1)}, u32[]{:S(2)}, u32[]{:S(2)}) collective-permute-start(bf16[64,3072]{1,0:T(8,128)(2,1)S(1)} %get-tuple-element.255), channel_id=1, source_target_pairs={{0,1},{1,2},{2,3},{4,5},{5,6},{6,7},{8,9},{9,10},{10,11},{12,13},{... | collective-permute-start | bytes 1179656 | tf_op jit(solution)/shard_map/ppermute | solution.py:452
  192.7 62.0 %collective-permute-start.58 = (bf16[64,3072]{1,0:T(8,128)(2,1)S(1)}, bf16[64,3072]{1,0:T(8,128)(2,1)S(1)}, u32[]{:S(2)}, u32[]{:S(2)}) collective-permute-start(bf16[64,3072]{1,0:T(8,128)(2,1)S(1)} %get-tuple-element.246), channel_id=1, source_target_pairs={{0,1},{1,2},{2,3},{4,5},{5,6},{6,7},{8,9},{9,10},{10,11},{12,13},{... | collective-permute-start | bytes 1179656 | tf_op jit(solution)/shard_map/ppermute | solution.py:458
  196.4 58.2 %collective-permute-start.59 = (bf16[64,3072]{1,0:T(8,128)(2,1)S(1)}, bf16[64,3072]{1,0:T(8,128)(2,1)S(1)}, u32[]{:S(2)}, u32[]{:S(2)}) collective-permute-start(bf16[64,3072]{1,0:T(8,128)(2,1)S(1)} %get-tuple-element.247), channel_id=1, source_target_pairs={{1,0},{2,1},{3,2},{5,4},{6,5},{7,6},{9,8},{10,9},{11,10},{13,12},{... | collective-permute-start | bytes 1179656 | tf_op jit(solution)/shard_map/ppermute | solution.py:459
  198.8 55.9 %collective-permute-start.56 = (bf16[64,3072]{1,0:T(8,128)(2,1)S(1)}, bf16[64,3072]{1,0:T(8,128)(2,1)S(1)}, u32[]{:S(2)}, u32[]{:S(2)}) collective-permute-start(bf16[64,3072]{1,0:T(8,128)(2,1)S(1)} %get-tuple-element.244), channel_id=1, source_target_pairs={{0,1},{1,2},{2,3},{4,5},{5,6},{6,7},{8,9},{9,10},{10,11},{12,13},{... | collective-permute-start | bytes 1179656 | tf_op jit(solution)/shard_map/ppermute | solution.py:458
  202.4 52.3 %collective-permute-start.57 = (bf16[64,3072]{1,0:T(8,128)(2,1)S(1)}, bf16[64,3072]{1,0:T(8,128)(2,1)S(1)}, u32[]{:S(2)}, u32[]{:S(2)}) collective-permute-start(bf16[64,3072]{1,0:T(8,128)(2,1)S(1)} %get-tuple-element.245), channel_id=1, source_target_pairs={{1,0},{2,1},{3,2},{5,4},{6,5},{7,6},{9,8},{10,9},{11,10},{13,12},{... | collective-permute-start | bytes 1179656 | tf_op jit(solution)/shard_map/ppermute | solution.py:459
  276.8 13.9 %collective-permute-start.60 = (bf16[64,3072]{1,0:T(8,128)(2,1)S(1)}, bf16[64,3072]{1,0:T(8,128)(2,1)S(1)}, u32[]{:S(2)}, u32[]{:S(2)}) collective-permute-start(bf16[64,3072]{1,0:T(8,128)(2,1)S(1)} %get-tuple-element.235), channel_id=1, source_target_pairs={{0,1},{4,5},{8,9},{12,13},{16,17},{20,21},{24,25},{28,29}} | collective-permute-start | bytes 1179656 | tf_op jit(solution)/shard_map/ppermute | solution.py:427
  278.2 18.5 %collective-permute-start.67 = (bf16[64,3072]{1,0:T(8,128)(2,1)S(1)}, bf16[64,3072]{1,0:T(8,128)(2,1)S(1)}, u32[]{:S(2)}, u32[]{:S(2)}) collective-permute-start(bf16[64,3072]{1,0:T(8,128)(2,1)S(1)} %get-tuple-element.240), channel_id=1, source_target_pairs={{3,2},{7,6},{11,10},{15,14},{19,18},{23,22},{27,26},{31,30}} | collective-permute-start | bytes 1179656 | tf_op jit(solution)/shard_map/ppermute | solution.py:428
  278.8 20.3 %collective-permute-start.66 = (bf16[64,3072]{1,0:T(8,128)(2,1)S(1)}, bf16[64,3072]{1,0:T(8,128)(2,1)S(1)}, u32[]{:S(2)}, u32[]{:S(2)}) collective-permute-start(bf16[64,3072]{1,0:T(8,128)(2,1)S(1)} %get-tuple-element.241), channel_id=1, source_target_pairs={{0,1},{4,5},{8,9},{12,13},{16,17},{20,21},{24,25},{28,29}} | collective-permute-start | bytes 1179656 | tf_op jit(solution)/shard_map/ppermute | solution.py:427
  290.8 14.3 %collective-permute-start.63 = (bf16[64,3072]{1,0:T(8,128)(2,1)S(1)}, bf16[64,3072]{1,0:T(8,128)(2,1)S(1)}, u32[]{:S(2)}, u32[]{:S(2)}) collective-permute-start(bf16[64,3072]{1,0:T(8,128)(2,1)S(1)} %get-tuple-element.232), channel_id=1, source_target_pairs={{2,1},{3,2},{6,5},{7,6},{10,9},{11,10},{14,13},{15,14},{18,17},{19... | collective-permute-start | bytes 1179656 | tf_op jit(solution)/shard_map/ppermute | solution.py:428
  292.1 15.5 %collective-permute-start.62 = (bf16[64,3072]{1,0:T(8,128)(2,1)S(1)}, bf16[64,3072]{1,0:T(8,128)(2,1)S(1)}, u32[]{:S(2)}, u32[]{:S(2)}) collective-permute-start(bf16[64,3072]{1,0:T(8,128)(2,1)S(1)} %get-tuple-element.233), channel_id=1, source_target_pairs={{0,1},{1,2},{4,5},{5,6},{8,9},{9,10},{12,13},{13,14},{16,17},{17,1... | collective-permute-start | bytes 1179656 | tf_op jit(solution)/shard_map/ppermute | solution.py:427
  299.2 14.5 %collective-permute-start.69 = (bf16[64,3072]{1,0:T(8,128)(2,1)S(1)}, bf16[64,3072]{1,0:T(8,128)(2,1)S(1)}, u32[]{:S(2)}, u32[]{:S(2)}) collective-permute-start(bf16[64,3072]{1,0:T(8,128)(2,1)S(1)} %get-tuple-element.238), channel_id=1, source_target_pairs={{2,1},{3,2},{6,5},{7,6},{10,9},{11,10},{14,13},{15,14},{18,17},{19... | collective-permute-start | bytes 1179656 | tf_op jit(solution)/shard_map/ppermute | solution.py:428
  300.5 15.5 %collective-permute-start.68 = (bf16[64,3072]{1,0:T(8,128)(2,1)S(1)}, bf16[64,3072]{1,0:T(8,128)(2,1)S(1)}, u32[]{:S(2)}, u32[]{:S(2)}) collective-permute-start(bf16[64,3072]{1,0:T(8,128)(2,1)S(1)} %get-tuple-element.239), channel_id=1, source_target_pairs={{0,1},{1,2},{4,5},{5,6},{8,9},{9,10},{12,13},{13,14},{16,17},{17,1... | collective-permute-start | bytes 1179656 | tf_op jit(solution)/shard_map/ppermute | solution.py:427
  307.7 16.1 %collective-permute-start.65 = (bf16[64,3072]{1,0:T(8,128)(2,1)S(1)}, bf16[64,3072]{1,0:T(8,128)(2,1)S(1)}, u32[]{:S(2)}, u32[]{:S(2)}) collective-permute-start(bf16[64,3072]{1,0:T(8,128)(2,1)S(1)} %get-tuple-element.230), channel_id=1, source_target_pairs={{1,0},{2,1},{3,2},{5,4},{6,5},{7,6},{9,8},{10,9},{11,10},{13,12},{... | collective-permute-start | bytes 1179656 | tf_op jit(solution)/shard_map/ppermute | solution.py:428
  309.8 14.7 %collective-permute-start.64 = (bf16[64,3072]{1,0:T(8,128)(2,1)S(1)}, bf16[64,3072]{1,0:T(8,128)(2,1)S(1)}, u32[]{:S(2)}, u32[]{:S(2)}) collective-permute-start(bf16[64,3072]{1,0:T(8,128)(2,1)S(1)} %get-tuple-element.231), channel_id=1, source_target_pairs={{0,1},{1,2},{2,3},{4,5},{5,6},{6,7},{8,9},{9,10},{10,11},{12,13},{... | collective-permute-start | bytes 1179656 | tf_op jit(solution)/shard_map/ppermute | solution.py:427
  (60 other events, 761.5 us)
